TPU v7x, 32 devices: a whole 2x2x4 slice. The times are simulated.
32 devices in a mesh: groups: 2 (over x), tile: 16 (over z, y, core).
Axes of the slice: x: 2, y: 2, z: 4, core: 2. Of those that a mesh axis runs over, the one named last changes fastest.
Arguments:
- image: float32 [4, 768, 4096], P(None, ('groups', 'tile')), parts along dimension 1, may hold values from -6 to 6
- inv_var: float32 [4, 768, 4096], P(None, ('groups', 'tile')), parts along dimension 1, may hold values from 0.25 to 4
- shift: float32 [8, 2], P('groups'), parts along dimension 0, may hold values from -0.5 to 0.5
- col_offset: int32 [8], P('groups'), parts along dimension 0, may hold values from -8 to 8
- psf_rows: float32 [8, 3, 41], P('groups'), parts along dimension 0, may hold values from -1 to 1
- psf_cols: float32 [8, 3, 41], P('groups'), parts along dimension 0, may hold values from -0.5 to 0.5
- placement: int32 [4096, 1], P(('groups', 'tile')), parts along dimension 0, may hold values from 0 to 15; in each aligned block of 128 rows (0 to 127, 128 to 255, ...) at most 16 rows name the same one
Outputs:
- matched: bfloat16 [4, 768, 4096], P(None, ('groups', 'tile')), parts along dimension 1
- coadd: float32 [32, 24, 128], P(('groups', 'tile')), parts along dimension 0
There are 2 independent parts, one for each index of `groups`. A program takes and returns all parts, laid end to end along the dimension named above; each array names one. Nothing has to cross between parts.
Inputs may be any that keep to these rules, and one draw needn't show every extreme that they name: `placement`: every patch receives at least one piece; within the pieces of one device no patch is named more than 16 times, a bound that some block reaches.
All inputs are finite; a program needn't handle non-finite values.
Results may differ from a plain program's by a relative error of at most 0.001.
Values sent between devices are 32-bit elements; how exact they have to be, the bound alone decides.
A program may use at most 192 MiB of HBM per device.

v0:
```python
import jax
import jax.numpy as jnp
from jax import lax
from jax.sharding import PartitionSpec as P

PC = 128


def padded_2(x, sides, width):
    for axis, dim in sides:
        size, length = (lax.axis_size(axis), x.shape[dim])
        up = [(i, (i + 1) % size) for i in range(size - 1)]
        down = [(j, i) for i, j in up]
        last = lax.slice_in_dim(x, length - width, length, axis=dim)
        leading = lax.slice_in_dim(x, 0, width, axis=dim)
        before = lax.ppermute(last, axis, up)
        after = lax.ppermute(leading, axis, down)
        x = jnp.concatenate([before, x, after], axis=dim)
    return x


def lanczos(values):
    return jnp.where(jnp.abs(values) < 3.0, jnp.sinc(values) * jnp.sinc(values / 3.0), 0.0)


def tap_weights(fraction):
    places = jnp.arange(-3, 4).astype(jnp.float32)
    weights = lanczos(places[None, :] + fraction[:, None])
    return weights / jnp.sum(weights, axis=1, keepdims=True)


def warp(extended, shift, col_offset):
    height = extended.shape[1] - 6
    width = extended.shape[2]
    row_weight = tap_weights(shift[:, 0])
    col_weight = tap_weights(shift[:, 1])
    shifted = jnp.zeros((extended.shape[0], height, width), jnp.float32)
    for place in range(-3, 4):
        shifted = (
            shifted
            + row_weight[:, place + 3, None, None] * extended[:, 3 - place : 3 - place + height]
        )
    padded = jnp.pad(shifted, ((0, 0), (0, 0), (11, 11)))

    def one_visit(plane, weights, offset):
        total = jnp.zeros((height, width), jnp.float32)
        for place in range(-3, 4):
            start = 11 - offset - place
            total = total + weights[place + 3] * lax.dynamic_slice_in_dim(plane, start, width, 1)
        return total

    return jax.vmap(one_visit)(padded, col_weight, col_offset)


def band_table(kernel, count):
    outer = jnp.arange(count, dtype=jnp.int32)[:, None]
    inner = jnp.arange(count + 40, dtype=jnp.int32)[None, :]
    index = outer + 40 - inner
    select = (index[:, :, None] == jnp.arange(41, dtype=jnp.int32)[None, None, :]).astype(
        jnp.float32
    )
    return jnp.einsum("vkt,oit->vkoi", kernel, select, precision=lax.Precision.HIGHEST)


def on_device(image, inv_var, shift, col_offset, psf_rows, psf_cols, placement):
    visits, height, width = image.shape
    raw = padded_2(image, (("tile", 1),), 3)
    warped = warp(raw, shift, col_offset)
    extended = padded_2(warped, (("tile", 1),), 20)
    row_band = band_table(psf_rows, height)
    along = jnp.einsum("vkim,vmw->vkiw", row_band, extended, precision=lax.Precision.HIGHEST)
    padded = jnp.pad(along, ((0, 0), (0, 0), (0, 0), (20, 20)))
    blocks = width // 128
    windows = jnp.stack(
        [padded[..., block * 128 : block * 128 + 168] for block in range(blocks)], axis=3
    )
    col_band = band_table(psf_cols, 128)
    matched = jnp.einsum("vkinw,vkow->vino", windows, col_band, precision=lax.Precision.HIGHEST)
    matched = matched.reshape(visits, height, width)
    pieces = width // PC
    labels = placement.reshape(visits, pieces)
    stacked = jnp.stack((inv_var * matched, inv_var)).reshape(2, visits, height, pieces, PC)
    owners = jnp.arange(1 * lax.axis_size("tile"), dtype=jnp.int32)
    onehot = (labels[None] == owners[:, None, None]).astype(jnp.float32)
    sums = lax.psum_scatter(
        jnp.einsum("pvc,svrcx->psrx", onehot, stacked, precision=lax.Precision.HIGHEST),
        "tile",
        scatter_dimension=0,
        tiled=True,
    )
    coadd = sums[:, 0] / jnp.maximum(sums[:, 1], 1.0)
    return (matched.astype(jnp.bfloat16), coadd)


def solution(mesh):
    in_specs = (
        P(None, ("groups", "tile"), None),
        P(None, ("groups", "tile"), None),
        P("groups", None),
        P("groups"),
        P("groups", None, None),
        P("groups", None, None),
        P(("groups", "tile"), None),
    )
    out_specs = (P(None, ("groups", "tile"), None), P(("groups", "tile"), None, None))
    return jax.shard_map(
        on_device, mesh=mesh, in_specs=in_specs, out_specs=out_specs, check_vma=False
    )
```

profile of v0, /device:TPU:0, one launch (start us, length us, event | category | flops | bytes accessed | tf_op | source)
XLA Modules:
  0.0 229.6 jit_solution(13277037182643720478)
XLA Ops:
  9.8 3.0 %collective-permute-start.1 = (f32[4,3,4096]{2,1,0:T(4,128)S(1)}, f32[4,3,4096]{2,1,0:T(4,128)S(1)}, u32[]{:S(2)}, u32[]{:S(2)}) collective-permute-start(f32[4,3,4096]{2,1,0:T(4,128)S(1)} %get-tuple-element.246), channel_id=1, source_target_pairs={{0,1},{1,2},{2,3},{3,4},{4,5},{5,6},{6,7},{7,8},{8,9},{9,10},{10,1... | collective-permute-start | bytes 589832 | tf_op jit(solution)/shard_map/ppermute | solution.py:16
  15.5 4.6 %fusion.15 = f32[4,24,4096]{2,1,0:T(8,128)S(1)} fusion(f32[4,24,4096]{2,1,0:T(8,128)} %param.8, f32[4,3,4096]{2,1,0:T(4,128)S(1)} %collective-permute-done.1, f32[4,27,4096]{2,1,0:T(8,128)S(1)} %constant_dynamic-update-slice_fusion, f32[4]{0:T(128)S(1)} %get-tuple-element.255, f32[4]{0:T(128)S(1)} %get-tuple-element.256, f32[4]{0:T(128)S(1)} %get-tuple-element.257, ...), kind=kLoop, calls=%fused_computation.37 | loop fusion | flops 6291456 | bytes 8061040 | tf_op jit(solution)/shard_map/add | solution.py:40
  20.8 8.1 %while.7 = (s32[]{:T(128)}, f32[4,24,4118]{2,1,0:T(8,128)S(1)}, s32[4,3]{1,0:T(4,128)S(1)}, f32[4,24,4096]{2,1,0:T(8,128)S(1)}, s32[]{:T(128)}) while((s32[]{:T(128)}, f32[4,24,4118]{2,1,0:T(8,128)S(1)}, s32[4,3]{1,0:T(4,128)S(1)}, f32[4,24,4096]{2,1,0:T(8,128)S(1)}, s32[]{:T(128)}) %tuple.183), condition=%wide.while_cond, body=%wide.while_body.sunk | while | flops 2 | bytes 786549 | solution.py:49
  30.6 10.8 %while.8 = (s32[]{:T(128)}, f32[4,24,4118]{2,1,0:T(8,128)S(1)}, s32[4,3]{1,0:T(4,128)S(1)}, f32[4,24,4096]{2,1,0:T(8,128)}, s32[]{:T(128)}) while((s32[]{:T(128)}, f32[4,24,4118]{2,1,0:T(8,128)S(1)}, s32[4,3]{1,0:T(4,128)S(1)}, f32[4,24,4096]{2,1,0:T(8,128)}, s32[]{:T(128)}) %tuple.188), condition=%wide.while_cond.1, body=%wide.while_body.1.sunk | while | flops 2 | bytes 788073 | solution.py:49
  31.1 2.1 dynamic-slice_dynamic-update-slice_fusion.15
  33.8 2.1 dynamic-slice_dynamic-update-slice_fusion.15
  36.5 2.1 dynamic-slice_dynamic-update-slice_fusion.15
  39.2 2.1 dynamic-slice_dynamic-update-slice_fusion.15
  41.4 8.5 %while.9 = (s32[]{:T(128)}, f32[4,24,4118]{2,1,0:T(8,128)S(1)}, s32[4,3]{1,0:T(4,128)S(1)}, f32[4,24,4096]{2,1,0:T(8,128)S(1)}, s32[]{:T(128)}) while((s32[]{:T(128)}, f32[4,24,4118]{2,1,0:T(8,128)S(1)}, s32[4,3]{1,0:T(4,128)S(1)}, f32[4,24,4096]{2,1,0:T(8,128)S(1)}, s32[]{:T(128)}) %tuple.189), condition=%wide.while_cond.2, body=%wide.while_body.2.sunk | while | flops 2 | bytes 786549 | solution.py:49
  51.7 11.4 %while.10 = (s32[]{:T(128)}, f32[4,24,4118]{2,1,0:T(8,128)S(1)}, s32[4,3]{1,0:T(4,128)S(1)}, f32[4,24,4096]{2,1,0:T(8,128)}, s32[]{:T(128)}) while((s32[]{:T(128)}, f32[4,24,4118]{2,1,0:T(8,128)S(1)}, s32[4,3]{1,0:T(4,128)S(1)}, f32[4,24,4096]{2,1,0:T(8,128)}, s32[]{:T(128)}) %tuple.190), condition=%wide.while_cond.3, body=%wide.while_body.3.sunk | while | flops 2 | bytes 788073 | solution.py:49
  52.3 2.2 dynamic-slice_dynamic-update-slice_fusion.17
  55.2 2.2 dynamic-slice_dynamic-update-slice_fusion.17
  58.1 2.2 dynamic-slice_dynamic-update-slice_fusion.17
  60.9 2.2 dynamic-slice_dynamic-update-slice_fusion.17
  63.2 8.2 %while.11 = (s32[]{:T(128)}, f32[4,24,4118]{2,1,0:T(8,128)S(1)}, s32[4,3]{1,0:T(4,128)S(1)}, f32[4,24,4096]{2,1,0:T(8,128)S(1)}, s32[]{:T(128)}) while((s32[]{:T(128)}, f32[4,24,4118]{2,1,0:T(8,128)S(1)}, s32[4,3]{1,0:T(4,128)S(1)}, f32[4,24,4096]{2,1,0:T(8,128)S(1)}, s32[]{:T(128)}) %tuple.191), condition=%wide.while_cond.4, body=%wide.while_body.4.sunk | while | flops 2 | bytes 786549 | solution.py:49
  73.2 11.4 %while.12 = (s32[]{:T(128)}, f32[4,24,4118]{2,1,0:T(8,128)S(1)}, s32[4,3]{1,0:T(4,128)S(1)}, f32[4,24,4096]{2,1,0:T(8,128)}, s32[]{:T(128)}) while((s32[]{:T(128)}, f32[4,24,4118]{2,1,0:T(8,128)S(1)}, s32[4,3]{1,0:T(4,128)S(1)}, f32[4,24,4096]{2,1,0:T(8,128)}, s32[]{:T(128)}) %tuple.192), condition=%wide.while_cond.5, body=%wide.while_body.5.sunk | while | flops 2 | bytes 788073 | solution.py:49
  73.8 2.2 dynamic-slice_dynamic-update-slice_fusion.19
  76.7 2.2 dynamic-slice_dynamic-update-slice_fusion.19
  79.5 2.2 dynamic-slice_dynamic-update-slice_fusion.19
  82.4 2.2 dynamic-slice_dynamic-update-slice_fusion.19
  84.7 8.3 %while.13 = (s32[]{:T(128)}, f32[4,24,4118]{2,1,0:T(8,128)S(1)}, s32[4,3]{1,0:T(4,128)S(1)}, f32[4,24,4096]{2,1,0:T(8,128)S(1)}, s32[]{:T(128)}) while((s32[]{:T(128)}, f32[4,24,4118]{2,1,0:T(8,128)S(1)}, s32[4,3]{1,0:T(4,128)S(1)}, f32[4,24,4096]{2,1,0:T(8,128)S(1)}, s32[]{:T(128)}) %tuple.193), condition=%wide.while_cond.6, body=%wide.while_body.6.sunk | while | flops 2 | bytes 786549 | solution.py:49
  94.2 5.4 %multiply_add_fusion = f32[4,24,4096]{2,1,0:T(8,128)S(1)} fusion(f32[4,24,4096]{2,1,0:T(8,128)} %copy-done.2, f32[4,24,4096]{2,1,0:T(8,128)} %get-tuple-element.50, f32[4,24,4096]{2,1,0:T(8,128)} %copy-done.5, f32[4,24,4096]{2,1,0:T(8,128)} %get-tuple-element.34, f32[4,24,4096]{2,1,0:T(8,128)} %copy-done.4, f32[4,24,4096]{2,1,0:T(8,128)} %get-tuple-element.18, ...), kind=kLoop, calls=%fused_computation.52 | loop fusion | flops 5111808 | bytes 12583024 | tf_op jit(solution)/shard_map/vmap()/add | solution.py:49
  99.9 1.9 copy.59
  101.8 8.1 %collective-permute-start.2 = (f32[4,20,4096]{2,0,1:T(4,128)}, f32[4,20,4096]{2,0,1:T(4,128)}, u32[]{:S(2)}, u32[]{:S(2)}) collective-permute-start(f32[4,20,4096]{2,0,1:T(4,128)} %copy.59), channel_id=1, source_target_pairs={{0,1},{1,2},{2,3},{3,4},{4,5},{5,6},{6,7},{7,8},{8,9},{9,10},{10,1... | collective-permute-start | bytes 3932168 | tf_op jit(solution)/shard_map/ppermute | solution.py:16
  109.9 1.9 copy.60
  113.6 4.8 %copy.73 = pred[128,168,41,1]{1,2,3,0:T(8,128)(4,1)} copy(pred[128,168,41,1]{0,1,2,3:T(8,128)(4,1)S(1)} %fusion.7) | data formatting | bytes 1763328 | tf_op jit(solution)/shard_map/eq | solution.py:59
  121.4 3.6 %convolution_bitcast_fusion = f32[4,3,128,168,1]{3,0,1,2,4:T(4,128)S(1)} fusion(pred[128,168,41,1]{1,2,3,0:T(8,128)(4,1)} %copy.73, f32[4,3,41]{2,0,1:T(4,128)S(1)} %copy-done), kind=kOutput, calls=%fused_computation.54 | convolution fusion | flops 126959616 | bytes 1915824 | tf_op jit(solution)/shard_map/vkt,oit->vkoi/dot_general | solution.py:62
  125.4 2.1 copy.61
  127.5 2.1 copy.62
  129.6 4.3 %fusion.2 = f32[4,3,24,4096]{3,2,1,0:T(8,128)S(1)} fusion(f32[4,20,4096]{2,1,0:T(8,128)S(1)} %copy.62, f32[4,24,4096]{2,1,0:T(8,128)S(1)} %multiply_add_fusion, f32[4,20,4096]{2,1,0:T(8,128)S(1)} %copy.61, f32[4,3,24,64]{3,0,1,2:T(4,128)S(1)} %convolution_bitcast_fusion.1), kind=kOutput, calls=%fused_computation.19 | convolution fusion | flops 908066816 | bytes 8986624 | tf_op jit(solution)/shard_map/vkim,vmw->vkiw/dot_general | solution.py:71
  138.5 8.6 %fusion.24 = f32[4,32,3,8,128]{4,3,2,1,0:T(8,128)S(1)} fusion(f32[4,3,128,168,1]{3,0,1,2,4:T(4,128)S(1)} %convolution_bitcast_fusion, f32[4,3,24,32,168]{4,2,1,0,3:T(8,128)S(1)} %fusion.37), kind=kOutput, calls=%fused_computation.53 | convolution fusion | flops 2378170368 | bytes 8798208 | tf_op jit(solution)/shard_map/vkinw,vkow->vino/dot_general | solution.py:78
  150.8 70.6 %reduce-scatter.2.cloned.1.call-done = f32[1,2,24,128]{3,2,1,0:T(8,128)} async-done(((f32[16,2,24,128]{3,2,1,0:T(8,128)}), f32[1,2,24,128]{3,2,1,0:T(8,128)}) %reduce-scatter.2.cloned.1.call-update) | async-done | bytes 24592 | tf_op jit(solution)/shard_map/reduce_scatter | solution.py:85
  (176 shorter events, 67.5 us)
Async XLA Ops:
  7.2 114.3 %copy-start = (f32[4,3,41]{2,0,1:T(4,128)S(1)}, f32[4,3,41]{2,0,1:T(4,128)}, u32[]{:S(2)}) copy-start(f32[4,3,41]{2,0,1:T(4,128)} %param.13) | copy-start | bytes 5908
  7.2 214.3 %reduce-scatter.2.cloned.1.call-start = ((), (), s32[]{:S(2)}) async-start(), calls=%async_computation.1 | async-start | bytes 417792 | tf_op jit(solution)/shard_map/reduce_scatter | solution.py:85
  8.5 5.9 %copy-start.7 = (f32[4,2]{0,1:T(2,128)S(1)}, f32[4,2]{0,1:T(2,128)}, u32[]{:S(2)}) copy-start(f32[4,2]{0,1:T(2,128)} %param.10) | copy-start | bytes 100
  8.5 6.1 %copy-start.8 = (s32[4]{0:T(128)S(1)}, s32[4]{0:T(128)}, u32[]{:S(2)}) copy-start(s32[4]{0:T(128)} %param.11) | copy-start | bytes 52
  8.5 6.8 %collective-permute-start = (f32[4,3,4096]{2,1,0:T(4,128)S(1)}, f32[4,3,4096]{2,1,0:T(4,128)S(1)}, u32[]{:S(2)}, u32[]{:S(2)}) collective-permute-start(f32[4,3,4096]{2,1,0:T(4,128)S(1)} %get-tuple-element.245), channel_id=1, source_target_pairs={{1,0},{2,1},{3,2},{4,3},{5,4},{6,5},{7,6},{8,7},{9,8},{10,9},{11,1... | collective-permute-start | bytes 589832 | tf_op jit(solution)/shard_map/ppermute | solution.py:17
  9.8 5.6 %collective-permute-start.1 = (f32[4,3,4096]{2,1,0:T(4,128)S(1)}, f32[4,3,4096]{2,1,0:T(4,128)S(1)}, u32[]{:S(2)}, u32[]{:S(2)}) collective-permute-start(f32[4,3,4096]{2,1,0:T(4,128)S(1)} %get-tuple-element.246), channel_id=1, source_target_pairs={{0,1},{1,2},{2,3},{3,4},{4,5},{5,6},{6,7},{7,8},{8,9},{9,10},{10,1... | collective-permute-start | bytes 589832 | tf_op jit(solution)/shard_map/ppermute | solution.py:16
  28.9 1.7 copy-start.3
  49.9 1.7 copy-start.4
  71.5 1.7 copy-start.5
  93.0 1.2 copy-start.2
  101.8 23.5 %collective-permute-start.2 = (f32[4,20,4096]{2,0,1:T(4,128)}, f32[4,20,4096]{2,0,1:T(4,128)}, u32[]{:S(2)}, u32[]{:S(2)}) collective-permute-start(f32[4,20,4096]{2,0,1:T(4,128)} %copy.59), channel_id=1, source_target_pairs={{0,1},{1,2},{2,3},{3,4},{4,5},{5,6},{6,7},{7,8},{8,9},{9,10},{10,1... | collective-permute-start | bytes 3932168 | tf_op jit(solution)/shard_map/ppermute | solution.py:16
  111.8 15.7 %collective-permute-start.3 = (f32[4,20,4096]{2,0,1:T(4,128)}, f32[4,20,4096]{2,0,1:T(4,128)}, u32[]{:S(2)}, u32[]{:S(2)}) collective-permute-start(f32[4,20,4096]{2,0,1:T(4,128)} %copy.60), channel_id=1, source_target_pairs={{1,0},{2,1},{3,2},{4,3},{5,4},{6,5},{7,6},{8,7},{9,8},{10,9},{11,1... | collective-permute-start | bytes 3932168 | tf_op jit(solution)/shard_map/ppermute | solution.py:17
  118.4 2.2 copy-start.9
  120.1 5.0 %copy-start.6 = (f32[4,3,41]{2,0,1:T(4,128)S(1)}, f32[4,3,41]{2,0,1:T(4,128)}, u32[]{:S(2)}) copy-start(f32[4,3,41]{2,0,1:T(4,128)} %param.12) | copy-start | bytes 5908
  138.5 8.7 %copy-start.1 = (f32[4,24,4096]{2,1,0:T(8,128)S(1)}, f32[4,24,4096]{2,1,0:T(8,128)}, u32[]{:S(2)}) copy-start(f32[4,24,4096]{2,1,0:T(8,128)} %param.9) | copy-start | bytes 4718596
Sparse Core Ops, SparseCore 0:
  149.9 71.4 reduce-scatter.1
where the time goes:
time: 231 us; the launch traced here: 230 us
  local copies, waits for them, and re-layouts  99 us (43%)
  waiting for transfers between devices  70.6 us (31%)
  matrix products  18.1 us (8%)
  between operations  14.7 us (6%)
  starting transfers between devices  13.7 us (6%)
  other arithmetic  13 us (6%)
    reduce_scatter x1, waiting for transfers between devices, on_device(): lax.psum_scatter(jnp.einsum('pvc,svrcx->psrx', onehot, stacked, precision...  70.6 us
    gather x84, local copies, waits for them, and re-layouts  66.2 us
    unnamed x70, local copies, waits for them, and re-layouts  15.8 us
    ppermute x2, starting transfers between devices, padded_2(): before = lax.ppermute(last, axis, up)  11.1 us
    dot_general x1, matrix products, on_device(): jnp.einsum('vkinw,vkow->vino', windows, col_band, precision=lax.Precision...  8.64 us
    add x1, other arithmetic, one_visit(): total + weights[place + 3] * lax.dynamic_slice_in_dim(plane, start, width...  5.38 us
    eq x1, local copies, waits for them, and re-layouts, band_table(): index[:, :, None] == jnp.arange(41, dtype=jnp.int32)[None, None, :]  4.76 us
    add x1, other arithmetic, warp(): shifted + row_weight[:, place + 3, None, None] * extended[:, 3 - place:3...  4.63 us
  transfers between devices with their start and end apart: 5, of which 1 were waited for; matrix products, arithmetic and copies ran while one was open for 9% of the time, Pallas kernels for 0%

commit v1 on v0

v1 whole, which is shorter than its diff:
```python
import functools

import jax
import jax.numpy as jnp
from jax import lax
from jax.experimental import pallas as pl
from jax.experimental.pallas import tpu as pltpu
from jax.sharding import PartitionSpec as P

PC = 128
LEAD = 20
BF = jnp.bfloat16
F32 = jnp.float32


def lanczos(values):
    return jnp.where(jnp.abs(values) < 3.0, jnp.sinc(values) * jnp.sinc(values / 3.0), 0.0)


def tap_weights(fraction):
    places = jnp.arange(-3, 4).astype(F32)
    weights = lanczos(places[None, :] + fraction[:, None])
    return weights / jnp.sum(weights, axis=1, keepdims=True)


def two_terms(x):
    high = x.astype(BF)
    return high, (x - high.astype(F32)).astype(BF)


def rounded_terms(x):
    high = lax.reduce_precision(x, exponent_bits=8, mantissa_bits=7)
    return high.astype(BF), (x - high).astype(BF)


def pick(weights, index):
    total = 0.0
    for t in range(weights.shape[1]):
        w = weights[:, t].reshape((-1,) + (1,) * (index.ndim - 1))
        total = total + jnp.where(index == t, w, 0.0)
    return total


def row_operator(row_tap, psf_rows, height, me, n):
    visits, terms, _ = psf_rows.shape
    i = jnp.arange(height, dtype=jnp.int32)[:, None, None]
    m = jnp.arange(height + 40, dtype=jnp.int32)[None, :, None]
    select = (i - m + 40 == jnp.arange(41, dtype=jnp.int32)[None, None, :]).astype(F32)
    band = jnp.einsum("vka,ima->vkim", psf_rows, select, precision=lax.Precision.HIGHEST)
    mi = jnp.arange(height + 40, dtype=jnp.int32)[:, None]
    ri = jnp.arange(3 * height, dtype=jnp.int32)[None, :]
    taps = pick(row_tap, (mi - ri + height - LEAD + 3)[None])
    row = me * height + mi - LEAD
    taps = jnp.where((row >= 0) & (row < n * height), taps, 0.0)
    full = jnp.einsum("vkim,vmr->vkir", band, taps, precision=lax.Precision.HIGHEST)
    full = full.reshape(visits, terms * height, 3 * height)
    high, low = rounded_terms(full)
    stacked = jnp.concatenate([high, high, low], axis=2)
    rows = -(-stacked.shape[1] // 16) * 16
    depth = -(-stacked.shape[2] // 256) * 256
    return jnp.pad(
        stacked, ((0, 0), (0, rows - stacked.shape[1]), (0, depth - stacked.shape[2]))
    )


def edge_operator(col_tap, col_offset, psf_cols):
    visits, terms, _ = psf_cols.shape
    m = jnp.arange(PC, dtype=jnp.int32)[:, None]
    j = jnp.arange(LEAD, dtype=jnp.int32)[None, :]
    place = jnp.stack([j - LEAD - m, PC + j - m])[None] - col_offset[:, None, None, None]
    taps = pick(col_tap, place + 3)
    jj = jnp.arange(LEAD, dtype=jnp.int32)[:, None]
    o = jnp.arange(PC, dtype=jnp.int32)[None, :]
    index = jnp.stack([o - jj + 40, o - PC - jj + 20])
    select = (index[..., None] == jnp.arange(41, dtype=jnp.int32)).astype(F32)
    psf = jnp.einsum("vkb,ejob->vkejo", psf_cols, select, precision=lax.Precision.HIGHEST)
    full = jnp.einsum("vemj,vkejo->vekmo", taps, psf, precision=lax.Precision.HIGHEST)
    high, low = rounded_terms(full.reshape(visits, 2, terms * PC, PC))
    return jnp.concatenate([high, low], axis=3)


def band_kernel(terms, c_ref, out_ref):
    for k in range(terms):
        row = jnp.broadcast_to(c_ref[0, k : k + 1, :], (PC, 2 * PC))
        turned = pltpu.roll(row, 0, 1, stride=1, stride_axis=0)
        m = lax.broadcasted_iota(jnp.int32, (PC, PC), 0)
        o = lax.broadcasted_iota(jnp.int32, (PC, PC), 1)
        far = turned[:, PC:]
        for d, part in enumerate(
            [jnp.where(o < m, far, 0.0), turned[:, :PC], jnp.where(o > m, far, 0.0)]
        ):
            high = part.astype(BF)
            low = (part - high.astype(F32)).astype(BF)
            start = (3 * k + d) * PC
            out_ref[0, start : start + PC, :PC] = high
            out_ref[0, start : start + PC, PC:] = low


def col_operator(col_tap, col_offset, psf_cols):
    visits, terms, _ = psf_cols.shape
    b = jnp.arange(41, dtype=jnp.int32)[:, None]
    lane = jnp.arange(2 * PC, dtype=jnp.int32)[None, :]
    signed = jnp.where(lane < PC, lane, lane - 2 * PC)
    spread = pick(col_tap, (signed - b + LEAD + 3)[None] - col_offset[:, None, None])
    line = jnp.einsum("vkb,vbl->vkl", psf_cols, spread, precision=lax.Precision.HIGHEST)
    return pl.pallas_call(
        functools.partial(band_kernel, terms),
        grid=(visits,),
        in_specs=[pl.BlockSpec((1, terms, 2 * PC), lambda v: (v, 0, 0))],
        out_specs=pl.BlockSpec((1, terms * 3 * PC, 2 * PC), lambda v: (v, 0, 0)),
        out_shape=jax.ShapeDtypeStruct((visits, terms * 3 * PC, 2 * PC), BF),
    )(line)


def split_dot(x, w_ref):
    high, low = two_terms(x)
    wide = jnp.dot(high, w_ref[...], preferred_element_type=F32)
    narrow = jnp.dot(low, w_ref[:, :PC], preferred_element_type=F32)
    return wide[:, :PC] + wide[:, PC:] + narrow


def main_kernel(
    n, terms, image, inv_var, rows_op, cols_op, edge_op, hot, out_m, out_c,
    halo, lines, block, sums, got, halo_send, halo_recv, sum_send, sum_recv,
):
    visits, height, width = image.shape
    pieces = width // PC
    me = lax.axis_index("tile")

    barrier = pltpu.get_barrier_semaphore()

    def greet(d, carry):
        pl.semaphore_signal(
            barrier, inc=1, device_id={"tile": lax.rem(me + d, n)},
            device_id_type=pl.DeviceIdType.MESH,
        )
        return carry

    lax.fori_loop(1, n, greet, 0)
    pl.semaphore_wait(barrier, n - 1)

    def halo_copy(v, side):
        other = me + 1 if side == 0 else me - 1
        return pltpu.make_async_remote_copy(
            src_ref=image.at[v], dst_ref=halo.at[side, v],
            send_sem=halo_send.at[side, v], recv_sem=halo_recv.at[side, v],
            device_id={"tile": other}, device_id_type=pl.DeviceIdType.MESH,
        )

    for v in range(visits):
        @pl.when(me < n - 1)
        def _():
            halo_copy(v, 0).start()

        @pl.when(me > 0)
        def _():
            halo_copy(v, 1).start()

    @pl.when(me == 0)
    def _():
        halo[0] = jnp.zeros_like(halo[0])

    @pl.when(me == n - 1)
    def _():
        halo[1] = jnp.zeros_like(halo[1])

    def add_up(v, which, first):
        def owner(p, carry):
            total = jnp.zeros((height, PC), F32) if first else sums[which, p]
            for c in range(pieces):
                total = total + hot[(v * pieces + c) * n + p] * block[c]
            sums[which, p] = total
            return carry

        lax.fori_loop(0, n, owner, 0)

    def sum_copy(which, d):
        return pltpu.make_async_remote_copy(
            src_ref=sums.at[which, lax.rem(me + d, n)], dst_ref=got.at[which, me],
            send_sem=sum_send.at[which, d], recv_sem=sum_recv.at[which, me],
            device_id={"tile": lax.rem(me + d, n)}, device_id_type=pl.DeviceIdType.MESH,
        )

    def send_sums(which):
        def one(d, carry):
            sum_copy(which, d).start()
            return carry

        lax.fori_loop(1, n, one, 0)

    for v in range(visits):
        for c in range(pieces):
            block[c] = inv_var[v, :, c * PC : (c + 1) * PC]
        add_up(v, 1, v == 0)
    send_sums(1)

    for k in range(terms):
        lines[k, 0] = jnp.zeros((height, PC), F32)
        lines[k, pieces + 1] = jnp.zeros((height, PC), F32)

    depth = rows_op.shape[2]
    step = 4
    for v in range(visits):
        @pl.when(me > 0)
        def _():
            pltpu.make_async_copy(image.at[v], halo.at[0, v], halo_recv.at[0, v]).wait()

        @pl.when(me < n - 1)
        def _():
            pltpu.make_async_copy(image.at[v], halo.at[1, v], halo_recv.at[1, v]).wait()

        def rows_stage(q, carry):
            cols = pl.ds(pl.multiple_of(q * (step * PC), step * PC), step * PC)
            x = jnp.concatenate([halo[0, v, :, cols], image[v, :, cols], halo[1, v, :, cols]], 0)
            high = x.astype(BF).astype(F32)
            rest = jnp.zeros((depth - 9 * height, step * PC), F32)
            stacked = jnp.concatenate([high, x - high, high, rest], 0).astype(BF)
            y = jnp.dot(rows_op[v], stacked, preferred_element_type=F32)
            for k in range(terms):
                for s in range(step):
                    lines[k, q * step + s + 1] = y[
                        k * height : (k + 1) * height, s * PC : (s + 1) * PC
                    ]
            return carry

        lax.fori_loop(0, pieces // step, rows_stage, 0)

        half = pieces // 2

        def cols_stage(q, carry):
            parts = [
                lines[k, pl.ds(q * half + d, half)].reshape(half * height, PC)
                for k in range(terms)
                for d in range(3)
            ]
            res = split_dot(jnp.concatenate(parts, 1), cols_op.at[v])
            block[pl.ds(q * half, half)] = res.reshape(half, height, PC)
            return carry

        lax.fori_loop(0, 2, cols_stage, 0)
        for e, c in ((0, 0), (1, pieces - 1)):
            x = jnp.concatenate([lines[k, c + 1] for k in range(terms)], 1)
            block[c] = block[c] - split_dot(x, edge_op.at[v, e])
        for c in range(pieces):
            cols = slice(c * PC, (c + 1) * PC)
            value = block[c]
            out_m[v, :, cols] = value.astype(BF)
            block[c] = value * inv_var[v, :, cols]
        add_up(v, 0, v == 0)
    send_sums(0)

    totals = []
    for which in (1, 0):
        def one(d, total):
            source = lax.rem(me + n - d, n)
            pltpu.make_async_copy(
                sums.at[which, 0], got.at[which, source], sum_recv.at[which, source]
            ).wait()
            return total + got[which, source]

        totals.append(lax.fori_loop(1, n, one, sums[which, me]))
    out_c[0] = totals[1] / jnp.maximum(totals[0], 1.0)

    for which in (0, 1):
        def done(d, carry):
            sum_copy(which, d).wait_send()
            return carry

        lax.fori_loop(1, n, done, 0)
    for v in range(visits):
        @pl.when(me < n - 1)
        def _():
            halo_copy(v, 0).wait_send()

        @pl.when(me > 0)
        def _():
            halo_copy(v, 1).wait_send()


def on_device(image, inv_var, shift, col_offset, psf_rows, psf_cols, placement):
    visits, height, width = image.shape
    n = lax.axis_size("tile")
    me = lax.axis_index("tile")
    terms = psf_rows.shape[1]
    pieces = width // PC
    row_tap = tap_weights(shift[:, 0])
    col_tap = tap_weights(shift[:, 1])
    rows_op = row_operator(row_tap, psf_rows, height, me, n)
    cols_op = col_operator(col_tap, col_offset, psf_cols)
    edge_op = edge_operator(col_tap, col_offset, psf_cols)
    hot = (placement == jnp.arange(n, dtype=jnp.int32)[None, :]).astype(F32).reshape(-1)
    vmem = pl.BlockSpec(memory_space=pltpu.VMEM)
    return pl.pallas_call(
        functools.partial(main_kernel, n, terms),
        out_shape=(
            jax.ShapeDtypeStruct((visits, height, width), BF),
            jax.ShapeDtypeStruct((1, height, PC), F32),
        ),
        in_specs=[vmem] * 5 + [pl.BlockSpec(memory_space=pltpu.SMEM)],
        out_specs=(vmem, vmem),
        scratch_shapes=[
            pltpu.VMEM((2, visits, height, width), F32),
            pltpu.VMEM((terms, pieces + 2, height, PC), F32),
            pltpu.VMEM((pieces, height, PC), F32),
            pltpu.VMEM((2, n, height, PC), F32),
            pltpu.VMEM((2, n, height, PC), F32),
            pltpu.SemaphoreType.DMA((2, visits)),
            pltpu.SemaphoreType.DMA((2, visits)),
            pltpu.SemaphoreType.DMA((2, n)),
            pltpu.SemaphoreType.DMA((2, n)),
        ],
        compiler_params=pltpu.CompilerParams(
            collective_id=0, has_side_effects=True, vmem_limit_bytes=48 * 1024 * 1024
        ),
    )(image, inv_var, rows_op, cols_op, edge_op, hot)


def solution(mesh):
    in_specs = (
        P(None, ("groups", "tile"), None),
        P(None, ("groups", "tile"), None),
        P("groups", None),
        P("groups"),
        P("groups", None, None),
        P("groups", None, None),
        P(("groups", "tile"), None),
    )
    out_specs = (P(None, ("groups", "tile"), None), P(("groups", "tile"), None, None))
    return jax.shard_map(
        on_device, mesh=mesh, in_specs=in_specs, out_specs=out_specs, check_vma=False
    )
```

time: 231 us -> 69.3 us (0.30)
  local copies, waits for them, and re-layouts: 99 us -> 3.77 us
  waiting for transfers between devices: 70.6 us -> 0 us
  Pallas kernels: 0 us -> 58.2 us
  between operations: 14.7 us -> 0.88 us
  starting transfers between devices: 13.7 us -> 0 us
  matrix products: 18.1 us -> 4.53 us
  other arithmetic: 13 us -> 1.6 us
    reduce_scatter x1 -> x0, waiting for transfers between devices: 70.6 us -> none  [on_device(): lax.psum_scatter(jnp.einsum('pvc,svrcx->psrx', onehot, stacked, precision...]
    gather x84 -> x0, local copies, waits for them, and re-layouts: 66.2 us -> none
    pallas_call x0 -> x2, Pallas kernels: none -> 58.2 us  [the longest x1 54.7 us: on_device(): pl.pallas_call(functools.partial(main_kernel, n, terms), out_shape=(jax.S...]
    ppermute x4 -> x0, starting transfers between devices: 13.7 us -> none  [the longest x2 11.1 us: padded_2(): before = lax.ppermute(last, axis, up)]
    dot_general x5, matrix products: 18.1 us -> 4.53 us  [the longest x1 1.69 us: col_operator(): jnp.einsum('vkb,vbl->vkl', psf_cols, spread, precision=lax.Precision.HIGH...]
    unnamed x70 -> x14, local copies, waits for them, and re-layouts: 15.8 us -> 2.92 us
    add x4, other arithmetic: 10 us -> 0.04 us  [the longest x1 0.02 us: edge_operator(): index = jnp.stack([o - jj + 40, o - PC - jj + 20])]
    slice x4 -> x0, local copies, waits for them, and re-layouts: 5.44 us -> none  [the longest x2 3.21 us: padded_2(): leading = lax.slice_in_dim(x, 0, width, axis=dim)]
  transfers between devices with their start and end apart: 5 -> 0, of which waited for: 1 -> 0; matrix products, arithmetic and copies ran while one was open for 9% -> 0% of each run, Pallas kernels for 0% -> 0%
where the time goes in v1:
time: 69.3 us; the launch traced here: 69 us
  Pallas kernels  58.2 us (84%)
  matrix products  4.53 us (7%)
  local copies, waits for them, and re-layouts  3.77 us (5%)
  other arithmetic  1.6 us (2%)
  between operations  0.88 us (1%)
    pallas_call x1, Pallas kernels, on_device(): pl.pallas_call(functools.partial(main_kernel, n, terms), out_shape=(jax.S...  54.7 us
    pallas_call x1, Pallas kernels, col_operator(): pl.pallas_call(functools.partial(band_kernel, terms), grid=(visits,), in_...  3.51 us
    unnamed x14, local copies, waits for them, and re-layouts  2.92 us
    dot_general x1, matrix products, col_operator(): jnp.einsum('vkb,vbl->vkl', psf_cols, spread, precision=lax.Precision.HIGH...  1.69 us
    dot_general x1, matrix products, edge_operator(): jnp.einsum('vemj,vkejo->vekmo', taps, psf, precision=lax.Precision.HIGHEST)  1.58 us

profile of v1, /device:TPU:0, one launch (start us, length us, event | category | flops | bytes accessed | tf_op | source)
XLA Modules:
  0.0 69.0 jit_solution(1007344337361301231)
XLA Ops:
  0.6 0.0 copy-start
  0.6 0.0 copy-start.4
  0.7 0.0 copy-start.3
  0.7 0.8 %slice_bitcast_fusion.15 = (f32[4]{0:T(128)S(1)}, f32[4]{0:T(128)S(1)}) fusion(f32[4,2]{0,1:T(2,128)} %param.10), kind=kLoop, calls=%fused_computation.300 | loop fusion | bytes 64 | tf_op jit(solution)/shard_map/add | solution.py:22
  1.5 0.1 fusion.226
  1.6 0.1 broadcast_divide_fusion
  1.9 0.1 iota_subtract_fusion
  2.0 0.0 copy-done
  2.0 1.7 %convolution_bitcast_fusion.2.c_ref = f32[4,3,256]{2,1,0:T(4,128)} fusion(f32[4]{0:T(128)S(1)} %get-tuple-element.10, f32[4]{0:T(128)S(1)} %get-tuple-element.11, f32[4]{0:T(128)S(1)} %get-tuple-element.12, f32[4]{0:T(128)S(1)} %get-tuple-element.13, f32[4]{0:T(128)S(1)} %get-tuple-element.14, f32[4]{0:T(128)S(1)} %get-tuple-element.15, ...), kind=kOutput, calls=%fused_computation.7 | convolution fusion | flops 2393088 | bytes 56368 | tf_op jit(solution)/shard_map/vkb,vbl->vkl/dot_general | solution.py:105
  3.7 0.0 copy-done.4
  3.7 0.0 copy-start.5
  3.7 0.1 fusion.101
  3.8 0.1 reshape.318.hot
  3.9 0.0 copy-done.3
  3.9 0.3 convolution_bitcast_fusion.1
  4.2 0.5 fusion.30
  4.8 0.1 fusion.28.rows_op
  4.9 0.4 compare_bitcast_fusion
  5.3 0.4 convolution_bitcast_fusion
  5.8 0.0 copy-done.5
  5.8 1.6 %fusion.8 = f32[4,2,3,128,128]{3,4,2,1,0:T(8,128)S(1)} fusion(f32[4,3,2,20,128]{4,0,1,3,2:T(4,128)S(1)} %convolution_bitcast_fusion, f32[4]{0:T(128)S(1)} %get-tuple-element.10, f32[4]{0:T(128)S(1)} %get-tuple-element.11, f32[4]{0:T(128)S(1)} %get-tuple-element.12, f32[4]{0:T(128)S(1)} %get-tuple-element.13, f32[4]{0:T(128)S(1)} %get-tuple-element.14, ...), kind=kOutput, calls=%fused_computation.24 | convolution fusion | flops 94822400 | bytes 1839232 | tf_op jit(solution)/shard_map/vemj,vkejo->vekmo/dot_general | solution.py:77
  7.4 0.3 reduce-precision_convert_fusion
  7.7 0.2 pad_maximum_fusion.edge_op
  7.9 0.0 copy-start.1
  7.9 3.5 %shard_map.86.cols_op = bf16[4,1152,256]{2,1,0:T(8,128)(2,1)} custom-call(f32[4,3,256]{2,1,0:T(4,128)} %convolution_bitcast_fusion.2.c_ref), custom_call_target="tpu_custom_call" | custom-call | tf_op jit(solution)/shard_map/pallas_call | solution.py:106
  11.4 0.0 copy-done.1
  11.4 0.0 copy-start.2
  11.4 1.4 %copy-done.2 = f32[4,24,4096]{2,1,0:T(8,128)S(1)} copy-done((f32[4,24,4096]{2,1,0:T(8,128)S(1)}, f32[4,24,4096]{2,1,0:T(8,128)}, u32[]{:S(2)}) %copy-start.2) | copy-done | bytes 1572888
  12.8 54.7 %shard_map.87 = (bf16[4,24,4096]{2,1,0:T(8,128)(2,1)S(1)}, f32[1,24,128]{2,1,0:T(8,128)S(1)}) custom-call(f32[4,24,4096]{2,1,0:T(8,128)S(1)} %copy-done.1, f32[4,24,4096]{2,1,0:T(8,128)S(1)} %copy-done.2, bf16[4,80,256]{2,1,0:T(8,128)(2,1)S(1)} %fusion.28.rows_op, bf16[4,1152,256]{2,1,0:T(8,128)(2,1)} %shard_map.86.cols_op, ...), custom_call_target="tpu_custom_call" | custom-call | tf_op jit(solution)/shard_map/pallas_call | solution.py:293
  67.5 0.9 %copy.32 = bf16[4,24,4096]{2,1,0:T(8,128)(2,1)} copy(bf16[4,24,4096]{2,1,0:T(8,128)(2,1)S(1)} %get-tuple-element.46) | data formatting | bytes 1572864
  68.4 0.6 copy.33
  (17 shorter events, 0.2 us)
Async XLA Ops:
  0.6 1.4 %copy-start = (f32[4,3,41]{2,0,1:T(4,128)S(1)}, f32[4,3,41]{2,0,1:T(4,128)}, u32[]{:S(2)}) copy-start(f32[4,3,41]{2,0,1:T(4,128)} %param.13) | copy-start | bytes 5908
  0.6 3.0 %copy-start.4 = (s32[128,1]{0,1:T(1,128)S(1)}, s32[128,1]{0,1:T(1,128)}, u32[]{:S(2)}) copy-start(s32[128,1]{0,1:T(1,128)} %param.14) | copy-start | bytes 1540
  0.7 3.2 %copy-start.3 = (f32[4,3,41]{2,0,1:T(4,128)S(1)}, f32[4,3,41]{2,0,1:T(4,128)}, u32[]{:S(2)}) copy-start(f32[4,3,41]{2,0,1:T(4,128)} %param.12) | copy-start | bytes 5908
  3.7 2.1 %copy-start.5 = (s32[4]{0:T(128)S(1)}, s32[4]{0:T(128)}, u32[]{:S(2)}) copy-start(s32[4]{0:T(128)} %param.11) | copy-start | bytes 52
  7.9 3.5 %copy-start.1 = (f32[4,24,4096]{2,1,0:T(8,128)S(1)}, f32[4,24,4096]{2,1,0:T(8,128)}, u32[]{:S(2)}) copy-start(f32[4,24,4096]{2,1,0:T(8,128)} %image.1) | copy-start | bytes 4718596
  11.4 1.4 %copy-start.2 = (f32[4,24,4096]{2,1,0:T(8,128)S(1)}, f32[4,24,4096]{2,1,0:T(8,128)}, u32[]{:S(2)}) copy-start(f32[4,24,4096]{2,1,0:T(8,128)} %inv_var.1) | copy-start | bytes 4718596

commit v2 on v1

--- a/solution.py
+++ b/solution.py
@@ -120,11 +120,12 @@
 
 
 def main_kernel(
-    n, terms, image, inv_var, rows_op, cols_op, edge_op, hot, out_m, out_c,
+    n, terms, image, before, after, inv_var, rows_op, cols_op, edge_op, hot, out_m, out_c,
     halo, lines, block, sums, got, halo_send, halo_recv, sum_send, sum_recv,
 ):
     visits, height, width = image.shape
     pieces = width // PC
+    early = before.shape[0]
     me = lax.axis_index("tile")
 
     barrier = pltpu.get_barrier_semaphore()
@@ -142,12 +143,12 @@
     def halo_copy(v, side):
         other = me + 1 if side == 0 else me - 1
         return pltpu.make_async_remote_copy(
-            src_ref=image.at[v], dst_ref=halo.at[side, v],
-            send_sem=halo_send.at[side, v], recv_sem=halo_recv.at[side, v],
+            src_ref=image.at[v], dst_ref=halo.at[side, v - early],
+            send_sem=halo_send.at[side, v - early], recv_sem=halo_recv.at[side, v - early],
             device_id={"tile": other}, device_id_type=pl.DeviceIdType.MESH,
         )
 
-    for v in range(visits):
+    for v in range(early, visits):
         @pl.when(me < n - 1)
         def _():
             halo_copy(v, 0).start()
@@ -201,17 +202,22 @@
     depth = rows_op.shape[2]
     step = 4
     for v in range(visits):
-        @pl.when(me > 0)
-        def _():
-            pltpu.make_async_copy(image.at[v], halo.at[0, v], halo_recv.at[0, v]).wait()
-
-        @pl.when(me < n - 1)
-        def _():
-            pltpu.make_async_copy(image.at[v], halo.at[1, v], halo_recv.at[1, v]).wait()
-
-        def rows_stage(q, carry):
+        if v < early:
+            above, below = before.at[v], after.at[v]
+        else:
+            above, below = halo.at[0, v - early], halo.at[1, v - early]
+
+            @pl.when(me > 0)
+            def _():
+                pltpu.make_async_copy(image.at[v], above, halo_recv.at[0, v - early]).wait()
+
+            @pl.when(me < n - 1)
+            def _():
+                pltpu.make_async_copy(image.at[v], below, halo_recv.at[1, v - early]).wait()
+
+        def rows_stage(q, carry, above=above, below=below, v=v):
             cols = pl.ds(pl.multiple_of(q * (step * PC), step * PC), step * PC)
-            x = jnp.concatenate([halo[0, v, :, cols], image[v, :, cols], halo[1, v, :, cols]], 0)
+            x = jnp.concatenate([above[:, cols], image[v, :, cols], below[:, cols]], 0)
             high = x.astype(BF).astype(F32)
             rest = jnp.zeros((depth - 9 * height, step * PC), F32)
             stacked = jnp.concatenate([high, x - high, high, rest], 0).astype(BF)
@@ -267,7 +273,7 @@
             return carry
 
         lax.fori_loop(1, n, done, 0)
-    for v in range(visits):
+    for v in range(early, visits):
         @pl.when(me < n - 1)
         def _():
             halo_copy(v, 0).wait_send()
@@ -283,6 +289,10 @@
     me = lax.axis_index("tile")
     terms = psf_rows.shape[1]
     pieces = width // PC
+    early = visits // 2
+    up = [(i, i + 1) for i in range(n - 1)]
+    before = lax.ppermute(image[:early], "tile", up)
+    after = lax.ppermute(image[:early], "tile", [(j, i) for i, j in up])
     row_tap = tap_weights(shift[:, 0])
     col_tap = tap_weights(shift[:, 1])
     rows_op = row_operator(row_tap, psf_rows, height, me, n)
@@ -296,23 +306,23 @@
             jax.ShapeDtypeStruct((visits, height, width), BF),
             jax.ShapeDtypeStruct((1, height, PC), F32),
         ),
-        in_specs=[vmem] * 5 + [pl.BlockSpec(memory_space=pltpu.SMEM)],
+        in_specs=[vmem] * 7 + [pl.BlockSpec(memory_space=pltpu.SMEM)],
         out_specs=(vmem, vmem),
         scratch_shapes=[
-            pltpu.VMEM((2, visits, height, width), F32),
+            pltpu.VMEM((2, visits - early, height, width), F32),
             pltpu.VMEM((terms, pieces + 2, height, PC), F32),
             pltpu.VMEM((pieces, height, PC), F32),
             pltpu.VMEM((2, n, height, PC), F32),
             pltpu.VMEM((2, n, height, PC), F32),
-            pltpu.SemaphoreType.DMA((2, visits)),
-            pltpu.SemaphoreType.DMA((2, visits)),
+            pltpu.SemaphoreType.DMA((2, visits - early)),
+            pltpu.SemaphoreType.DMA((2, visits - early)),
             pltpu.SemaphoreType.DMA((2, n)),
             pltpu.SemaphoreType.DMA((2, n)),
         ],
         compiler_params=pltpu.CompilerParams(
             collective_id=0, has_side_effects=True, vmem_limit_bytes=48 * 1024 * 1024
         ),
-    )(image, inv_var, rows_op, cols_op, edge_op, hot)
+    )(image, before, after, inv_var, rows_op, cols_op, edge_op, hot)
 
 
 def solution(mesh):

time: 69.3 us -> 62.3 us (0.90)
  Pallas kernels: 58.2 us -> 46.2 us
  starting transfers between devices: 0 us -> 4.37 us
  other arithmetic: 1.6 us -> 2.73 us
    pallas_call x1, Pallas kernels: 54.7 us -> 42.7 us  [on_device(): pl.pallas_call(functools.partial(main_kernel, n, terms), out_shape=(jax.S...]
    ppermute x0 -> x2, starting transfers between devices: none -> 4.37 us  [the longest x1 3.08 us: on_device(): before = lax.ppermute(image[:early], 'tile', up)]
    slice x0 -> x1, local copies, waits for them, and re-layouts: none -> 1.21 us  [on_device(): before = lax.ppermute(image[:early], 'tile', up)]
    concatenate x1, other arithmetic: 0.19 us -> 1.32 us  [edge_operator(): return jnp.concatenate([high, low], axis=3)]
    add x1, local copies, waits for them, and re-layouts: 0.76 us -> 0.01 us  [tap_weights(): weights = lanczos(places[None, :] + fraction[:, None])]
    unnamed x14 -> x16, local copies, waits for them, and re-layouts: 2.92 us -> 2.62 us
  transfers between devices with their start and end apart: 0 -> 2, of which waited for: 0 -> 0; matrix products, arithmetic and copies ran while one was open for 0% -> 11% of each run, Pallas kernels for 0% -> 5%
where the time goes in v2:
time: 62.3 us; the launch traced here: 62 us
  Pallas kernels  46.2 us (74%)
  starting transfers between devices  4.37 us (7%)
  local copies, waits for them, and re-layouts  3.93 us (6%)
  matrix products  3.87 us (6%)
  other arithmetic  2.73 us (4%)
  between operations  0.95 us (2%)
    pallas_call x1, Pallas kernels, on_device(): pl.pallas_call(functools.partial(main_kernel, n, terms), out_shape=(jax.S...  42.7 us
    pallas_call x1, Pallas kernels, col_operator(): pl.pallas_call(functools.partial(band_kernel, terms), grid=(visits,), in_...  3.41 us
    ppermute x1, starting transfers between devices, on_device(): before = lax.ppermute(image[:early], 'tile', up)  3.08 us
    unnamed x16, local copies, waits for them, and re-layouts  2.62 us
    dot_general x1, matrix products, edge_operator(): jnp.einsum('vemj,vkejo->vekmo', taps, psf, precision=lax.Precision.HIGHEST)  1.58 us
    concatenate x1, other arithmetic, edge_operator(): return jnp.concatenate([high, low], axis=3)  1.32 us
    ppermute x1, starting transfers between devices, on_device(): after = lax.ppermute(image[:early], 'tile', [(j, i) for i, j in up])  1.29 us
  transfers between devices with their start and end apart: 2, of which 0 were waited for; matrix products, arithmetic and copies ran while one was open for 11% of the time, Pallas kernels for 5%

profile of v2, /device:TPU:0, one launch (start us, length us, event | category | flops | bytes accessed | tf_op | source)
XLA Modules:
  0.0 62.0 jit_solution(10812312155041505231)
XLA Ops:
  0.6 0.0 copy-start
  0.6 0.0 copy-start.4
  0.7 1.2 %slice.59 = f32[2,24,4096]{2,1,0:T(8,128)S(1)} slice(f32[4,24,4096]{2,1,0:T(8,128)} %image.1), slice={[0:2], [0:24], [0:4096]} | slice | bytes 1572864 | tf_op jit(solution)/shard_map/slice | solution.py:294
  1.9 0.0 copy-start.6
  1.9 1.3 %collective-permute-start.1 = (f32[2,24,4096]{2,1,0:T(8,128)S(1)}, f32[2,24,4096]{2,1,0:T(8,128)S(1)}, u32[]{:S(2)}, u32[]{:S(2)}) collective-permute-start(f32[2,24,4096]{2,1,0:T(8,128)S(1)} %slice.59), channel_id=1, source_target_pairs={{1,0},{2,1},{3,2},{4,3},{5,4},{6,5},{7,6},{8,7},{9,8},{10,9},{11,1... | collective-permute-start | bytes 2359304 | tf_op jit(solution)/shard_map/ppermute | solution.py:295
  3.2 3.1 %collective-permute-start = (f32[2,24,4096]{2,1,0:T(8,128)S(1)}, f32[2,24,4096]{2,1,0:T(8,128)S(1)}, u32[]{:S(2)}, u32[]{:S(2)}) collective-permute-start(f32[2,24,4096]{2,1,0:T(8,128)S(1)} %slice.59), channel_id=1, source_target_pairs={{0,1},{1,2},{2,3},{3,4},{4,5},{5,6},{6,7},{7,8},{8,9},{9,10},{10,1... | collective-permute-start | bytes 2359304 | tf_op jit(solution)/shard_map/ppermute | solution.py:294
  6.5 0.0 copy-done.5
  6.5 0.1 fusion.101
  6.6 0.1 reshape.318.hot
  6.7 0.1 fusion.226
  6.8 0.1 broadcast_divide_fusion
  6.9 0.0 copy-done.3
  7.0 0.3 convolution_bitcast_fusion.1
  7.3 0.5 fusion.30
  7.9 0.4 compare_bitcast_fusion
  8.3 0.4 convolution_bitcast_fusion
  8.8 1.0 %convolution_bitcast_fusion.2.c_ref = f32[4,3,256]{2,1,0:T(4,128)} fusion(f32[4]{0:T(128)S(1)} %get-tuple-element.10, f32[4]{0:T(128)S(1)} %get-tuple-element.11, f32[4]{0:T(128)S(1)} %get-tuple-element.12, f32[4]{0:T(128)S(1)} %get-tuple-element.13, f32[4]{0:T(128)S(1)} %get-tuple-element.14, f32[4]{0:T(128)S(1)} %get-tuple-element.15, ...), kind=kOutput, calls=%fused_computation.7 | convolution fusion | flops 2393088 | bytes 56368 | tf_op jit(solution)/shard_map/vkb,vbl->vkl/dot_general | solution.py:105
  9.8 3.4 %shard_map.86.cols_op = bf16[4,1152,256]{2,1,0:T(8,128)(2,1)} custom-call(f32[4,3,256]{2,1,0:T(4,128)} %convolution_bitcast_fusion.2.c_ref), custom_call_target="tpu_custom_call" | custom-call | tf_op jit(solution)/shard_map/pallas_call | solution.py:106
  13.2 0.1 iota_subtract_fusion
  13.3 0.1 fusion.28.rows_op
  13.4 1.6 %fusion.8 = f32[4,2,3,128,128]{3,4,2,1,0:T(8,128)S(1)} fusion(f32[4,3,2,20,128]{4,0,1,3,2:T(4,128)S(1)} %convolution_bitcast_fusion, f32[4]{0:T(128)S(1)} %get-tuple-element.10, f32[4]{0:T(128)S(1)} %get-tuple-element.11, f32[4]{0:T(128)S(1)} %get-tuple-element.12, f32[4]{0:T(128)S(1)} %get-tuple-element.13, f32[4]{0:T(128)S(1)} %get-tuple-element.14, ...), kind=kOutput, calls=%fused_computation.24 | convolution fusion | flops 94822400 | bytes 1839232 | tf_op jit(solution)/shard_map/vemj,vkejo->vekmo/dot_general | solution.py:77
  15.0 0.3 reduce-precision_convert_fusion
  15.3 0.0 copy-start.1
  15.3 0.0 copy-start.2
  15.3 1.3 %pad_maximum_fusion.edge_op = bf16[4,2,384,256]{3,2,1,0:T(8,128)(2,1)} fusion(bf16[4,2,384,128]{3,2,1,0:T(8,128)(2,1)S(1)} %get-tuple-element.6, bf16[4,2,384,128]{3,2,1,0:T(8,128)(2,1)S(1)} %get-tuple-element.5), kind=kLoop, calls=%fused_computation.4 | loop fusion | flops 3145728 | bytes 3145728 | tf_op jit(solution)/shard_map/concatenate | solution.py:79
  16.7 0.0 collective-permute-done.1.after
  16.7 0.0 collective-permute-done.before
  16.7 0.6 %copy-done.1 = f32[4,24,4096]{2,1,0:T(8,128)S(1)} copy-done((f32[4,24,4096]{2,1,0:T(8,128)S(1)}, f32[4,24,4096]{2,1,0:T(8,128)}, u32[]{:S(2)}) %copy-start.1) | copy-done | bytes 1572888
  17.3 0.5 copy-done.2
  17.8 42.7 %shard_map.87 = (bf16[4,24,4096]{2,1,0:T(8,128)(2,1)S(1)}, f32[1,24,128]{2,1,0:T(8,128)S(1)}) custom-call(f32[4,24,4096]{2,1,0:T(8,128)S(1)} %copy-done.1, f32[2,24,4096]{2,1,0:T(8,128)S(1)} %collective-permute-done.before, f32[2,24,4096]{2,1,0:T(8,128)S(1)} %collective-permute-done.1.after, f32[4,24,4096]{2,1,0:T(8,128)S(1)} %copy-done.2, ...), custom_call_target="tpu_custom_call" | custom-call | tf_op jit(solution)/shard_map/pallas_call | solution.py:303
  60.5 0.9 %copy.32 = bf16[4,24,4096]{2,1,0:T(8,128)(2,1)} copy(bf16[4,24,4096]{2,1,0:T(8,128)(2,1)S(1)} %get-tuple-element.46) | data formatting | bytes 1572864
  61.4 0.6 copy.33
  (23 shorter events, 0.2 us)
Async XLA Ops:
  0.6 7.7 %copy-start = (f32[4,3,41]{2,0,1:T(4,128)S(1)}, f32[4,3,41]{2,0,1:T(4,128)}, u32[]{:S(2)}) copy-start(f32[4,3,41]{2,0,1:T(4,128)} %param.13) | copy-start | bytes 5908
  0.6 5.8 %copy-start.4 = (f32[4,2]{0,1:T(2,128)S(1)}, f32[4,2]{0,1:T(2,128)}, u32[]{:S(2)}) copy-start(f32[4,2]{0,1:T(2,128)} %param.10) | copy-start | bytes 100
  0.7 5.9 %copy-start.5 = (s32[128,1]{0,1:T(1,128)S(1)}, s32[128,1]{0,1:T(1,128)}, u32[]{:S(2)}) copy-start(s32[128,1]{0,1:T(1,128)} %param.14) | copy-start | bytes 1540
  0.7 6.3 %copy-start.3 = (f32[4,3,41]{2,0,1:T(4,128)S(1)}, f32[4,3,41]{2,0,1:T(4,128)}, u32[]{:S(2)}) copy-start(f32[4,3,41]{2,0,1:T(4,128)} %param.12) | copy-start | bytes 5908
  1.9 6.9 %copy-start.6 = (s32[4]{0:T(128)S(1)}, s32[4]{0:T(128)}, u32[]{:S(2)}) copy-start(s32[4]{0:T(128)} %param.11) | copy-start | bytes 52
  1.9 14.8 %collective-permute-start.1 = (f32[2,24,4096]{2,1,0:T(8,128)S(1)}, f32[2,24,4096]{2,1,0:T(8,128)S(1)}, u32[]{:S(2)}, u32[]{:S(2)}) collective-permute-start(f32[2,24,4096]{2,1,0:T(8,128)S(1)} %slice.59), channel_id=1, source_target_pairs={{1,0},{2,1},{3,2},{4,3},{5,4},{6,5},{7,6},{8,7},{9,8},{10,9},{11,1... | collective-permute-start | bytes 2359304 | tf_op jit(solution)/shard_map/ppermute | solution.py:295
  3.2 13.5 %collective-permute-start = (f32[2,24,4096]{2,1,0:T(8,128)S(1)}, f32[2,24,4096]{2,1,0:T(8,128)S(1)}, u32[]{:S(2)}, u32[]{:S(2)}) collective-permute-start(f32[2,24,4096]{2,1,0:T(8,128)S(1)} %slice.59), channel_id=1, source_target_pairs={{0,1},{1,2},{2,3},{3,4},{4,5},{5,6},{6,7},{7,8},{8,9},{9,10},{10,1... | collective-permute-start | bytes 2359304 | tf_op jit(solution)/shard_map/ppermute | solution.py:294
  15.3 2.0 %copy-start.1 = (f32[4,24,4096]{2,1,0:T(8,128)S(1)}, f32[4,24,4096]{2,1,0:T(8,128)}, u32[]{:S(2)}) copy-start(f32[4,24,4096]{2,1,0:T(8,128)} %image.1) | copy-start | bytes 4718596
  15.3 2.4 %copy-start.2 = (f32[4,24,4096]{2,1,0:T(8,128)S(1)}, f32[4,24,4096]{2,1,0:T(8,128)}, u32[]{:S(2)}) copy-start(f32[4,24,4096]{2,1,0:T(8,128)} %inv_var.1) | copy-start | bytes 4718596

commit v3 on v2

--- a/solution.py
+++ b/solution.py
@@ -166,14 +166,23 @@
         halo[1] = jnp.zeros_like(halo[1])
 
     def add_up(v, which, first):
-        def owner(p, carry):
-            total = jnp.zeros((height, PC), F32) if first else sums[which, p]
+        group = 8 if n % 8 == 0 else 1
+
+        def owners(q, carry):
+            p = q * group
+            totals = [
+                jnp.zeros((height, PC), F32) if first else sums[which, p + g]
+                for g in range(group)
+            ]
             for c in range(pieces):
-                total = total + hot[(v * pieces + c) * n + p] * block[c]
-            sums[which, p] = total
-            return carry
-
-        lax.fori_loop(0, n, owner, 0)
+                piece = block[c]
+                for g in range(group):
+                    totals[g] = totals[g] + hot[(v * pieces + c) * n + p + g] * piece
+            for g in range(group):
+                sums[which, p + g] = totals[g]
+            return carry
+
+        lax.fori_loop(0, n // group, owners, 0)
 
     def sum_copy(which, d):
         return pltpu.make_async_remote_copy(

time: 62.3 us -> 63 us (1.011)
  Pallas kernels: 46.2 us -> 46.9 us
    pallas_call x1, Pallas kernels: 42.7 us -> 43.5 us  [on_device(): pl.pallas_call(functools.partial(main_kernel, n, terms), out_shape=(jax.S...]
where the time goes in v3:
time: 63 us; the launch traced here: 62.7 us
  Pallas kernels  46.9 us (74%)
  starting transfers between devices  4.37 us (7%)
  local copies, waits for them, and re-layouts  3.93 us (6%)
  matrix products  3.87 us (6%)
  other arithmetic  2.73 us (4%)
  between operations  0.95 us (2%)
    pallas_call x1, Pallas kernels, on_device(): pl.pallas_call(functools.partial(main_kernel, n, terms), out_shape=(jax.S...  43.5 us
    pallas_call x1, Pallas kernels, col_operator(): pl.pallas_call(functools.partial(band_kernel, terms), grid=(visits,), in_...  3.41 us
    ppermute x1, starting transfers between devices, on_device(): before = lax.ppermute(image[:early], 'tile', up)  3.08 us
    unnamed x16, local copies, waits for them, and re-layouts  2.62 us
    dot_general x1, matrix products, edge_operator(): jnp.einsum('vemj,vkejo->vekmo', taps, psf, precision=lax.Precision.HIGHEST)  1.58 us
    concatenate x1, other arithmetic, edge_operator(): return jnp.concatenate([high, low], axis=3)  1.32 us
    ppermute x1, starting transfers between devices, on_device(): after = lax.ppermute(image[:early], 'tile', [(j, i) for i, j in up])  1.29 us
  transfers between devices with their start and end apart: 2, of which 0 were waited for; matrix products, arithmetic and copies ran while one was open for 11% of the time, Pallas kernels for 5%

profile of v3, /device:TPU:0, one launch (start us, length us, event | category | flops | bytes accessed | tf_op | source)
XLA Modules:
  0.0 62.7 jit_solution(10235652588482293256)
XLA Ops:
  0.6 0.0 copy-start
  0.6 0.0 copy-start.4
  0.7 1.2 %slice.59 = f32[2,24,4096]{2,1,0:T(8,128)S(1)} slice(f32[4,24,4096]{2,1,0:T(8,128)} %image.1), slice={[0:2], [0:24], [0:4096]} | slice | bytes 1572864 | tf_op jit(solution)/shard_map/slice | solution.py:303
  1.9 0.0 copy-start.6
  1.9 1.3 %collective-permute-start.1 = (f32[2,24,4096]{2,1,0:T(8,128)S(1)}, f32[2,24,4096]{2,1,0:T(8,128)S(1)}, u32[]{:S(2)}, u32[]{:S(2)}) collective-permute-start(f32[2,24,4096]{2,1,0:T(8,128)S(1)} %slice.59), channel_id=1, source_target_pairs={{1,0},{2,1},{3,2},{4,3},{5,4},{6,5},{7,6},{8,7},{9,8},{10,9},{11,1... | collective-permute-start | bytes 2359304 | tf_op jit(solution)/shard_map/ppermute | solution.py:304
  3.2 3.1 %collective-permute-start = (f32[2,24,4096]{2,1,0:T(8,128)S(1)}, f32[2,24,4096]{2,1,0:T(8,128)S(1)}, u32[]{:S(2)}, u32[]{:S(2)}) collective-permute-start(f32[2,24,4096]{2,1,0:T(8,128)S(1)} %slice.59), channel_id=1, source_target_pairs={{0,1},{1,2},{2,3},{3,4},{4,5},{5,6},{6,7},{7,8},{8,9},{9,10},{10,1... | collective-permute-start | bytes 2359304 | tf_op jit(solution)/shard_map/ppermute | solution.py:303
  6.5 0.0 copy-done.5
  6.5 0.1 fusion.101
  6.6 0.1 reshape.318.hot
  6.7 0.1 fusion.226
  6.8 0.1 broadcast_divide_fusion
  7.0 0.3 convolution_bitcast_fusion.1
  7.3 0.5 fusion.30
  7.9 0.4 compare_bitcast_fusion
  8.3 0.0 copy-done
  8.3 0.4 convolution_bitcast_fusion
  8.8 1.0 %convolution_bitcast_fusion.2.c_ref = f32[4,3,256]{2,1,0:T(4,128)} fusion(f32[4]{0:T(128)S(1)} %get-tuple-element.10, f32[4]{0:T(128)S(1)} %get-tuple-element.11, f32[4]{0:T(128)S(1)} %get-tuple-element.12, f32[4]{0:T(128)S(1)} %get-tuple-element.13, f32[4]{0:T(128)S(1)} %get-tuple-element.14, f32[4]{0:T(128)S(1)} %get-tuple-element.15, ...), kind=kOutput, calls=%fused_computation.7 | convolution fusion | flops 2393088 | bytes 56368 | tf_op jit(solution)/shard_map/vkb,vbl->vkl/dot_general | solution.py:105
  9.8 3.4 %shard_map.86.cols_op = bf16[4,1152,256]{2,1,0:T(8,128)(2,1)} custom-call(f32[4,3,256]{2,1,0:T(4,128)} %convolution_bitcast_fusion.2.c_ref), custom_call_target="tpu_custom_call" | custom-call | tf_op jit(solution)/shard_map/pallas_call | solution.py:106
  13.2 0.1 iota_subtract_fusion
  13.3 0.1 fusion.28.rows_op
  13.4 1.6 %fusion.8 = f32[4,2,3,128,128]{3,4,2,1,0:T(8,128)S(1)} fusion(f32[4,3,2,20,128]{4,0,1,3,2:T(4,128)S(1)} %convolution_bitcast_fusion, f32[4]{0:T(128)S(1)} %get-tuple-element.10, f32[4]{0:T(128)S(1)} %get-tuple-element.11, f32[4]{0:T(128)S(1)} %get-tuple-element.12, f32[4]{0:T(128)S(1)} %get-tuple-element.13, f32[4]{0:T(128)S(1)} %get-tuple-element.14, ...), kind=kOutput, calls=%fused_computation.24 | convolution fusion | flops 94822400 | bytes 1839232 | tf_op jit(solution)/shard_map/vemj,vkejo->vekmo/dot_general | solution.py:77
  15.0 0.3 reduce-precision_convert_fusion
  15.3 0.0 copy-start.1
  15.3 0.0 copy-start.2
  15.3 1.3 %pad_maximum_fusion.edge_op = bf16[4,2,384,256]{3,2,1,0:T(8,128)(2,1)} fusion(bf16[4,2,384,128]{3,2,1,0:T(8,128)(2,1)S(1)} %get-tuple-element.6, bf16[4,2,384,128]{3,2,1,0:T(8,128)(2,1)S(1)} %get-tuple-element.5), kind=kLoop, calls=%fused_computation.4 | loop fusion | flops 3145728 | bytes 3145728 | tf_op jit(solution)/shard_map/concatenate | solution.py:79
  16.7 0.0 collective-permute-done.1.after
  16.7 0.0 collective-permute-done.before
  16.7 0.6 %copy-done.1 = f32[4,24,4096]{2,1,0:T(8,128)S(1)} copy-done((f32[4,24,4096]{2,1,0:T(8,128)S(1)}, f32[4,24,4096]{2,1,0:T(8,128)}, u32[]{:S(2)}) %copy-start.1) | copy-done | bytes 1572888
  17.3 0.5 copy-done.2
  17.8 43.5 %shard_map.87 = (bf16[4,24,4096]{2,1,0:T(8,128)(2,1)S(1)}, f32[1,24,128]{2,1,0:T(8,128)S(1)}) custom-call(f32[4,24,4096]{2,1,0:T(8,128)S(1)} %copy-done.1, f32[2,24,4096]{2,1,0:T(8,128)S(1)} %collective-permute-done.before, f32[2,24,4096]{2,1,0:T(8,128)S(1)} %collective-permute-done.1.after, f32[4,24,4096]{2,1,0:T(8,128)S(1)} %copy-done.2, ...), custom_call_target="tpu_custom_call" | custom-call | tf_op jit(solution)/shard_map/pallas_call | solution.py:312
  61.3 0.9 %copy.32 = bf16[4,24,4096]{2,1,0:T(8,128)(2,1)} copy(bf16[4,24,4096]{2,1,0:T(8,128)(2,1)S(1)} %get-tuple-element.46) | data formatting | bytes 1572864
  62.1 0.6 copy.33
  (23 shorter events, 0.2 us)
Async XLA Ops:
  0.6 7.7 %copy-start = (f32[4,3,41]{2,0,1:T(4,128)S(1)}, f32[4,3,41]{2,0,1:T(4,128)}, u32[]{:S(2)}) copy-start(f32[4,3,41]{2,0,1:T(4,128)} %param.13) | copy-start | bytes 5908
  0.6 5.8 %copy-start.4 = (f32[4,2]{0,1:T(2,128)S(1)}, f32[4,2]{0,1:T(2,128)}, u32[]{:S(2)}) copy-start(f32[4,2]{0,1:T(2,128)} %param.10) | copy-start | bytes 100
  0.7 5.9 %copy-start.5 = (s32[128,1]{0,1:T(1,128)S(1)}, s32[128,1]{0,1:T(1,128)}, u32[]{:S(2)}) copy-start(s32[128,1]{0,1:T(1,128)} %param.14) | copy-start | bytes 1540
  0.7 6.3 %copy-start.3 = (f32[4,3,41]{2,0,1:T(4,128)S(1)}, f32[4,3,41]{2,0,1:T(4,128)}, u32[]{:S(2)}) copy-start(f32[4,3,41]{2,0,1:T(4,128)} %param.12) | copy-start | bytes 5908
  1.9 6.9 %copy-start.6 = (s32[4]{0:T(128)S(1)}, s32[4]{0:T(128)}, u32[]{:S(2)}) copy-start(s32[4]{0:T(128)} %param.11) | copy-start | bytes 52
  1.9 14.8 %collective-permute-start.1 = (f32[2,24,4096]{2,1,0:T(8,128)S(1)}, f32[2,24,4096]{2,1,0:T(8,128)S(1)}, u32[]{:S(2)}, u32[]{:S(2)}) collective-permute-start(f32[2,24,4096]{2,1,0:T(8,128)S(1)} %slice.59), channel_id=1, source_target_pairs={{1,0},{2,1},{3,2},{4,3},{5,4},{6,5},{7,6},{8,7},{9,8},{10,9},{11,1... | collective-permute-start | bytes 2359304 | tf_op jit(solution)/shard_map/ppermute | solution.py:304
  3.2 13.5 %collective-permute-start = (f32[2,24,4096]{2,1,0:T(8,128)S(1)}, f32[2,24,4096]{2,1,0:T(8,128)S(1)}, u32[]{:S(2)}, u32[]{:S(2)}) collective-permute-start(f32[2,24,4096]{2,1,0:T(8,128)S(1)} %slice.59), channel_id=1, source_target_pairs={{0,1},{1,2},{2,3},{3,4},{4,5},{5,6},{6,7},{7,8},{8,9},{9,10},{10,1... | collective-permute-start | bytes 2359304 | tf_op jit(solution)/shard_map/ppermute | solution.py:303
  15.3 2.0 %copy-start.1 = (f32[4,24,4096]{2,1,0:T(8,128)S(1)}, f32[4,24,4096]{2,1,0:T(8,128)}, u32[]{:S(2)}) copy-start(f32[4,24,4096]{2,1,0:T(8,128)} %image.1) | copy-start | bytes 4718596
  15.3 2.4 %copy-start.2 = (f32[4,24,4096]{2,1,0:T(8,128)S(1)}, f32[4,24,4096]{2,1,0:T(8,128)}, u32[]{:S(2)}) copy-start(f32[4,24,4096]{2,1,0:T(8,128)} %inv_var.1) | copy-start | bytes 4718596

commit v4 on v2

--- a/solution.py
+++ b/solution.py
@@ -289,7 +289,7 @@
     me = lax.axis_index("tile")
     terms = psf_rows.shape[1]
     pieces = width // PC
-    early = visits // 2
+    early = visits - 1
     up = [(i, i + 1) for i in range(n - 1)]
     before = lax.ppermute(image[:early], "tile", up)
     after = lax.ppermute(image[:early], "tile", [(j, i) for i, j in up])

time: 62.3 us -> 69.7 us (1.12)
  other arithmetic: 2.73 us -> 15.9 us
  Pallas kernels: 46.2 us -> 36.6 us
  matrix products: 3.87 us -> 6.19 us
  local copies, waits for them, and re-layouts: 3.93 us -> 4.99 us
    pallas_call x1, Pallas kernels: 42.7 us -> 33.2 us  [on_device(): pl.pallas_call(functools.partial(main_kernel, n, terms), out_shape=(jax.S...]
    eq x4, other arithmetic: 0.06 us -> 2.43 us  [pick(): total = total + jnp.where(index == t, w, 0.0)]
    convert_element_type x1, other arithmetic: 0.08 us -> 1.37 us  [on_device(): (placement == jnp.arange(n, dtype=jnp.int32)[None, :]).astype(F32)]
    add x1, other arithmetic: 0.02 us -> 1.28 us  [edge_operator(): index = jnp.stack([o - jj + 40, o - PC - jj + 20])]
    concatenate x1, other arithmetic: 0.13 us -> 1.1 us  [row_operator(): stacked = jnp.concatenate([high, high, low], axis=2)]
    convert_element_type x1, local copies, waits for them, and re-layouts: 0.08 us -> 0.92 us  [on_device(): (placement == jnp.arange(n, dtype=jnp.int32)[None, :]).astype(F32)]
    dot_general x1, matrix products: 1.03 us -> 1.84 us  [col_operator(): jnp.einsum('vkb,vbl->vkl', psf_cols, spread, precision=lax.Precision.HIGH...]
    dot_general x1, matrix products: 0.53 us -> 1.33 us  [row_operator(): jnp.einsum('vkim,vmr->vkir', band, taps, precision=lax.Precision.HIGHEST)]
  transfers between devices with their start and end apart: 2 -> 2, of which waited for: 0 -> 0; matrix products, arithmetic and copies ran while one was open for 11% -> 34% of each run, Pallas kernels for 5% -> 5%
where the time goes in v4:
time: 69.7 us; the launch traced here: 69 us
  Pallas kernels  36.6 us (53%)
  other arithmetic  15.9 us (23%)
  matrix products  6.19 us (9%)
  local copies, waits for them, and re-layouts  4.99 us (7%)
  starting transfers between devices  4.4 us (6%)
  between operations  0.97 us (1%)
    pallas_call x1, Pallas kernels, on_device(): pl.pallas_call(functools.partial(main_kernel, n, terms), out_shape=(jax.S...  33.2 us
    pallas_call x1, Pallas kernels, col_operator(): pl.pallas_call(functools.partial(band_kernel, terms), grid=(visits,), in_...  3.42 us
    ppermute x1, starting transfers between devices, on_device(): before = lax.ppermute(image[:early], 'tile', up)  3.11 us
    eq x4, other arithmetic, pick(): total = total + jnp.where(index == t, w, 0.0)  2.43 us
    unnamed x38, local copies, waits for them, and re-layouts  2.18 us
    dot_general x1, matrix products, col_operator(): jnp.einsum('vkb,vbl->vkl', psf_cols, spread, precision=lax.Precision.HIGH...  1.84 us
    dot_general x1, matrix products, edge_operator(): jnp.einsum('vemj,vkejo->vekmo', taps, psf, precision=lax.Precision.HIGHEST)  1.58 us
  transfers between devices with their start and end apart: 2, of which 0 were waited for; matrix products, arithmetic and copies ran while one was open for 34% of the time, Pallas kernels for 5%

profile of v4, /device:TPU:0, one launch (start us, length us, event | category | flops | bytes accessed | tf_op | source)
XLA Modules:
  0.0 69.0 jit_solution(13604786752681040643)
XLA Ops:
  0.7 1.4 %slice.59 = f32[3,24,4096]{2,1,0:T(8,128)S(1)} slice(f32[4,24,4096]{2,1,0:T(8,128)} %image.1), slice={[0:3], [0:24], [0:4096]} | slice | bytes 2359296 | tf_op jit(solution)/shard_map/slice | solution.py:294
  2.0 1.3 %collective-permute-start.1 = (f32[3,24,4096]{2,1,0:T(8,128)S(1)}, f32[3,24,4096]{2,1,0:T(8,128)S(1)}, u32[]{:S(2)}, u32[]{:S(2)}) collective-permute-start(f32[3,24,4096]{2,1,0:T(8,128)S(1)} %slice.59), channel_id=1, source_target_pairs={{1,0},{2,1},{3,2},{4,3},{5,4},{6,5},{7,6},{8,7},{9,8},{10,9},{11,1... | collective-permute-start | bytes 3538952 | tf_op jit(solution)/shard_map/ppermute | solution.py:295
  3.3 3.1 %collective-permute-start = (f32[3,24,4096]{2,1,0:T(8,128)S(1)}, f32[3,24,4096]{2,1,0:T(8,128)S(1)}, u32[]{:S(2)}, u32[]{:S(2)}) collective-permute-start(f32[3,24,4096]{2,1,0:T(8,128)S(1)} %slice.59), channel_id=1, source_target_pairs={{0,1},{1,2},{2,3},{3,4},{4,5},{5,6},{6,7},{7,8},{8,9},{9,10},{10,1... | collective-permute-start | bytes 3538952 | tf_op jit(solution)/shard_map/ppermute | solution.py:294
  6.4 0.6 add_convert_fusion
  8.0 0.5 iota_add_fusion
  8.6 0.6 fusion.132
  9.2 0.6 subtract_add_fusion.3
  9.8 0.6 fusion.130
  10.4 0.6 fusion.128
  11.0 0.6 fusion.126
  11.6 0.6 compare_and_fusion
  12.2 0.5 slice_bitcast_fusion.15
  12.7 1.3 %subtract_add_fusion.4 = (s32[1,20,128]{2,0,1:T(1,128)}, s32[1,20,128]{2,0,1:T(1,128)}) fusion(s32[128]{0:T(128)} %iota_add_fusion.2), kind=kLoop, calls=%fused_computation.175 | loop fusion | flops 10240 | bytes 20992 | tf_op jit(solution)/shard_map/add | solution.py:74
  14.0 0.6 subtract_add_fusion.1
  14.6 1.4 %fusion.101 = f32[128,16]{1,0:T(8,128)} fusion(s32[128]{0:T(128)} %bitcast.72), kind=kLoop, calls=%fused_computation.114 | loop fusion | flops 4096 | bytes 8704 | tf_op jit(solution)/shard_map/convert_element_type | solution.py:301
  16.0 0.9 %reshape.318.hot = f32[2048]{0:T(1024)S(1)} reshape(f32[128,16]{1,0:T(8,128)} %fusion.101) | data formatting | bytes 16384 | tf_op jit(solution)/shard_map/convert_element_type | solution.py:301
  16.9 0.8 %fusion.226 = (f32[4]{0:T(128)S(1)}, f32[4]{0:T(128)S(1)}) fusion(f32[4]{0:T(128)} %get-tuple-element.24, f32[7]{0:T(128)} %add_convert_fusion, f32[4]{0:T(128)} %get-tuple-element.23), kind=kLoop, calls=%fused_computation.279 | loop fusion | flops 4024 | bytes 92 | tf_op jit(solution)/shard_map/reduce_sum | solution.py:23
  17.7 0.8 %broadcast_divide_fusion = (f32[4,7]{0,1:T(8,128)S(1)}, f32[4,7]{0,1:T(8,128)S(1)}) fusion(f32[4]{0:T(128)S(1)} %get-tuple-element.3, f32[4]{0:T(128)} %get-tuple-element.24, f32[7]{0:T(128)} %add_convert_fusion, f32[4]{0:T(128)S(1)} %get-tuple-element.4, f32[4]{0:T(128)} %get-tuple-element.23), kind=kLoop, calls=%fused_computation.277 | loop fusion | flops 4032 | bytes 316 | tf_op jit(solution)/shard_map/div | solution.py:23
  18.5 1.0 %convolution_bitcast_fusion.1 = f32[4,3,24,64]{3,0,1,2:T(4,128)S(1)} fusion(s32[24,64]{1,0:T(8,128)} %subtract_add_fusion.3, f32[4,3,41]{2,0,1:T(4,128)} %param.12), kind=kOutput, calls=%fused_computation.6 | convolution fusion | flops 9131520 | bytes 81840 | tf_op jit(solution)/shard_map/vka,ima->vkim/dot_general | solution.py:49
  19.6 1.3 %fusion.30 = f32[4,3,24,72]{3,2,1,0:T(8,128)S(1)} fusion(f32[4,3,24,64]{3,0,1,2:T(4,128)S(1)} %convolution_bitcast_fusion.1, f32[4]{0:T(128)S(1)} %get-tuple-element.32, f32[4]{0:T(128)S(1)} %get-tuple-element.31, f32[4]{0:T(128)S(1)} %get-tuple-element.30, f32[4]{0:T(128)S(1)} %get-tuple-element.29, f32[4]{0:T(128)S(1)} %get-tuple-element.28, ...), kind=kOutput, calls=%fused_computation.48 | convolution fusion | flops 16183296 | bytes 189104 | tf_op jit(solution)/shard_map/vkim,vmr->vkir/dot_general | solution.py:55
  20.9 0.7 reduce-precision_convert_fusion.1
  21.7 1.8 %convolution_bitcast_fusion.2.c_ref = f32[4,3,256]{2,1,0:T(4,128)} fusion(f32[4]{0:T(128)S(1)} %get-tuple-element.10, f32[4]{0:T(128)S(1)} %get-tuple-element.11, f32[4]{0:T(128)S(1)} %get-tuple-element.12, f32[4]{0:T(128)S(1)} %get-tuple-element.13, f32[4]{0:T(128)S(1)} %get-tuple-element.14, f32[4]{0:T(128)S(1)} %get-tuple-element.15, ...), kind=kOutput, calls=%fused_computation.7 | convolution fusion | flops 2393088 | bytes 56368 | tf_op jit(solution)/shard_map/vkb,vbl->vkl/dot_general | solution.py:105
  23.5 3.4 %shard_map.86.cols_op = bf16[4,1152,256]{2,1,0:T(8,128)(2,1)} custom-call(f32[4,3,256]{2,1,0:T(4,128)} %convolution_bitcast_fusion.2.c_ref), custom_call_target="tpu_custom_call" | custom-call | tf_op jit(solution)/shard_map/pallas_call | solution.py:106
  27.0 0.7 %pad_add_fusion.1 = s32[2,20,128]{2,0,1:T(2,128)S(1)} fusion(s32[1,20,128]{2,0,1:T(1,128)} %get-tuple-element.40, s32[1,20,128]{2,0,1:T(1,128)} %get-tuple-element.41), kind=kLoop, calls=%fused_computation.149 | loop fusion | flops 5120 | bytes 40960 | tf_op jit(solution)/shard_map/stack | solution.py:74
  27.7 0.7 %iota_subtract_fusion = (s32[1,128,20]{1,2,0:T(8,128)S(1)}, s32[1,128,20]{1,2,0:T(8,128)S(1)}) fusion(s32[20]{0:T(128)} %iota_add_fusion, s32[20]{0:T(128)} %iota_add_fusion.1), kind=kLoop, calls=%fused_computation.162 | loop fusion | flops 5120 | bytes 20640 | tf_op jit(solution)/shard_map/sub | solution.py:70
  28.4 1.1 %fusion.28.rows_op = bf16[4,80,256]{2,1,0:T(8,128)(2,1)S(1)} fusion(bf16[4,72,72]{2,1,0:T(8,128)(2,1)} %get-tuple-element.8, bf16[4,72,72]{2,1,0:T(8,128)(2,1)} %get-tuple-element.7), kind=kLoop, calls=%fused_computation.46 | loop fusion | flops 1228800 | bytes 246784 | tf_op jit(solution)/shard_map/concatenate | solution.py:58
  30.5 1.6 %fusion.8 = f32[4,2,3,128,128]{3,4,2,1,0:T(8,128)S(1)} fusion(f32[4,3,2,20,128]{4,0,1,3,2:T(4,128)S(1)} %convolution_bitcast_fusion, f32[4]{0:T(128)S(1)} %copy-done.5, f32[4]{0:T(128)S(1)} %copy-done.7, f32[4]{0:T(128)S(1)} %copy-done.9, f32[4]{0:T(128)S(1)} %copy-done.11, f32[4]{0:T(128)S(1)} %copy-done.13, f32[4]{0:T(128)S(1)} %copy-done.15, ...), kind=kOutput, calls=%fused_computation.24 | convolution fusion | flops 94822400 | bytes 1839232 | tf_op jit(solution)/shard_map/vemj,vkejo->vekmo/dot_general | solution.py:77
  32.4 1.3 %pad_maximum_fusion.edge_op = bf16[4,2,384,256]{3,2,1,0:T(8,128)(2,1)} fusion(bf16[4,2,384,128]{3,2,1,0:T(8,128)(2,1)S(1)} %get-tuple-element.6, bf16[4,2,384,128]{3,2,1,0:T(8,128)(2,1)S(1)} %get-tuple-element.5), kind=kLoop, calls=%fused_computation.4 | loop fusion | flops 3145728 | bytes 3145728 | tf_op jit(solution)/shard_map/concatenate | solution.py:79
  33.7 0.6 copy-done.1
  34.3 33.2 %shard_map.87 = (bf16[4,24,4096]{2,1,0:T(8,128)(2,1)S(1)}, f32[1,24,128]{2,1,0:T(8,128)S(1)}) custom-call(f32[4,24,4096]{2,1,0:T(8,128)S(1)} %copy-done.1, f32[3,24,4096]{2,1,0:T(8,128)S(1)} %collective-permute-done.before, f32[3,24,4096]{2,1,0:T(8,128)S(1)} %collective-permute-done.1.after, f32[4,24,4096]{2,1,0:T(8,128)} %inv_var.1, ...), custom_call_target="tpu_custom_call" | custom-call | tf_op jit(solution)/shard_map/pallas_call | solution.py:303
  67.6 0.9 %copy.32 = bf16[4,24,4096]{2,1,0:T(8,128)(2,1)} copy(bf16[4,24,4096]{2,1,0:T(8,128)(2,1)S(1)} %get-tuple-element.46) | data formatting | bytes 1572864
  68.5 0.6 copy.33
  (45 shorter events, 2.3 us)
Async XLA Ops:
  0.6 21.0 %copy-start = (f32[4,3,41]{2,0,1:T(4,128)S(1)}, f32[4,3,41]{2,0,1:T(4,128)}, u32[]{:S(2)}) copy-start(f32[4,3,41]{2,0,1:T(4,128)} %param.13) | copy-start | bytes 5908
  0.6 11.5 %copy-start.16 = (f32[4,2]{0,1:T(2,128)S(1)}, f32[4,2]{0,1:T(2,128)}, u32[]{:S(2)}) copy-start(f32[4,2]{0,1:T(2,128)} %param.10) | copy-start | bytes 100
  2.0 31.7 %collective-permute-start.1 = (f32[3,24,4096]{2,1,0:T(8,128)S(1)}, f32[3,24,4096]{2,1,0:T(8,128)S(1)}, u32[]{:S(2)}, u32[]{:S(2)}) collective-permute-start(f32[3,24,4096]{2,1,0:T(8,128)S(1)} %slice.59), channel_id=1, source_target_pairs={{1,0},{2,1},{3,2},{4,3},{5,4},{6,5},{7,6},{8,7},{9,8},{10,9},{11,1... | collective-permute-start | bytes 3538952 | tf_op jit(solution)/shard_map/ppermute | solution.py:295
  3.3 30.4 %collective-permute-start = (f32[3,24,4096]{2,1,0:T(8,128)S(1)}, f32[3,24,4096]{2,1,0:T(8,128)S(1)}, u32[]{:S(2)}, u32[]{:S(2)}) collective-permute-start(f32[3,24,4096]{2,1,0:T(8,128)S(1)} %slice.59), channel_id=1, source_target_pairs={{0,1},{1,2},{2,3},{3,4},{4,5},{5,6},{6,7},{7,8},{8,9},{9,10},{10,1... | collective-permute-start | bytes 3538952 | tf_op jit(solution)/shard_map/ppermute | solution.py:294
  18.5 3.1 %copy-start.2 = (f32[4]{0:T(128)}, f32[4]{0:T(128)S(1)}, u32[]{:S(2)}) copy-start(f32[4]{0:T(128)S(1)} %get-tuple-element.9) | copy-start | bytes 52
  18.5 3.1 %copy-start.4 = (f32[4]{0:T(128)}, f32[4]{0:T(128)S(1)}, u32[]{:S(2)}) copy-start(f32[4]{0:T(128)S(1)} %get-tuple-element.10) | copy-start | bytes 52
  18.5 3.1 %copy-start.6 = (f32[4]{0:T(128)}, f32[4]{0:T(128)S(1)}, u32[]{:S(2)}) copy-start(f32[4]{0:T(128)S(1)} %get-tuple-element.11) | copy-start | bytes 52
  18.5 3.1 %copy-start.8 = (f32[4]{0:T(128)}, f32[4]{0:T(128)S(1)}, u32[]{:S(2)}) copy-start(f32[4]{0:T(128)S(1)} %get-tuple-element.12) | copy-start | bytes 52
  18.5 3.1 %copy-start.10 = (f32[4]{0:T(128)}, f32[4]{0:T(128)S(1)}, u32[]{:S(2)}) copy-start(f32[4]{0:T(128)S(1)} %get-tuple-element.13) | copy-start | bytes 52
  18.5 3.1 %copy-start.12 = (f32[4]{0:T(128)}, f32[4]{0:T(128)S(1)}, u32[]{:S(2)}) copy-start(f32[4]{0:T(128)S(1)} %get-tuple-element.14) | copy-start | bytes 52
  18.5 3.1 %copy-start.14 = (f32[4]{0:T(128)}, f32[4]{0:T(128)S(1)}, u32[]{:S(2)}) copy-start(f32[4]{0:T(128)S(1)} %get-tuple-element.15) | copy-start | bytes 52
  26.9 3.5 %copy-start.3 = (f32[4]{0:T(128)S(1)}, f32[4]{0:T(128)}, u32[]{:S(2)}) copy-start(f32[4]{0:T(128)} %copy-done.2) | copy-start | bytes 52
  26.9 3.5 %copy-start.5 = (f32[4]{0:T(128)S(1)}, f32[4]{0:T(128)}, u32[]{:S(2)}) copy-start(f32[4]{0:T(128)} %copy-done.4) | copy-start | bytes 52
  26.9 3.5 %copy-start.7 = (f32[4]{0:T(128)S(1)}, f32[4]{0:T(128)}, u32[]{:S(2)}) copy-start(f32[4]{0:T(128)} %copy-done.6) | copy-start | bytes 52
  26.9 3.5 %copy-start.9 = (f32[4]{0:T(128)S(1)}, f32[4]{0:T(128)}, u32[]{:S(2)}) copy-start(f32[4]{0:T(128)} %copy-done.8) | copy-start | bytes 52
  26.9 3.5 %copy-start.11 = (f32[4]{0:T(128)S(1)}, f32[4]{0:T(128)}, u32[]{:S(2)}) copy-start(f32[4]{0:T(128)} %copy-done.10) | copy-start | bytes 52
  26.9 3.5 %copy-start.13 = (f32[4]{0:T(128)S(1)}, f32[4]{0:T(128)}, u32[]{:S(2)}) copy-start(f32[4]{0:T(128)} %copy-done.12) | copy-start | bytes 52
  26.9 3.5 %copy-start.15 = (f32[4]{0:T(128)S(1)}, f32[4]{0:T(128)}, u32[]{:S(2)}) copy-start(f32[4]{0:T(128)} %copy-done.14) | copy-start | bytes 52
  27.0 3.5 %copy-start.17 = (s32[4]{0:T(128)S(1)}, s32[4]{0:T(128)}, u32[]{:S(2)}) copy-start(s32[4]{0:T(128)} %param.11) | copy-start | bytes 52
  32.4 2.0 %copy-start.1 = (f32[4,24,4096]{2,1,0:T(8,128)S(1)}, f32[4,24,4096]{2,1,0:T(8,128)}, u32[]{:S(2)}) copy-start(f32[4,24,4096]{2,1,0:T(8,128)} %image.1) | copy-start | bytes 4718596

commit v5 on v4

--- a/solution.py
+++ b/solution.py
@@ -289,7 +289,7 @@
     me = lax.axis_index("tile")
     terms = psf_rows.shape[1]
     pieces = width // PC
-    early = visits - 1
+    early = max(1, visits // 4)
     up = [(i, i + 1) for i in range(n - 1)]
     before = lax.ppermute(image[:early], "tile", up)
     after = lax.ppermute(image[:early], "tile", [(j, i) for i, j in up])

time: 69.7 us -> 68.7 us (0.986)
  Pallas kernels: 36.6 us -> 50.7 us
  other arithmetic: 15.9 us -> 3.38 us
  matrix products: 6.19 us -> 4.56 us
    pallas_call x1, Pallas kernels: 33.2 us -> 47.3 us  [on_device(): pl.pallas_call(functools.partial(main_kernel, n, terms), out_shape=(jax.S...]
    eq x4, other arithmetic: 2.43 us -> 0.06 us  [pick(): total = total + jnp.where(index == t, w, 0.0)]
    add x1, other arithmetic: 1.28 us -> 0.02 us  [edge_operator(): index = jnp.stack([o - jj + 40, o - PC - jj + 20])]
    concatenate x1, other arithmetic: 1.1 us -> 0.13 us  [row_operator(): stacked = jnp.concatenate([high, high, low], axis=2)]
    convert_element_type x1, local copies, waits for them, and re-layouts: 0.92 us -> 0.08 us  [on_device(): (placement == jnp.arange(n, dtype=jnp.int32)[None, :]).astype(F32)]
    dot_general x1, matrix products: 1.84 us -> 1.03 us  [col_operator(): jnp.einsum('vkb,vbl->vkl', psf_cols, spread, precision=lax.Precision.HIGH...]
    dot_general x1, matrix products: 1.33 us -> 0.53 us  [row_operator(): jnp.einsum('vkim,vmr->vkir', band, taps, precision=lax.Precision.HIGHEST)]
    another operation x1, other arithmetic: 0.74 us -> 0.02 us  [edge_operator(): index = jnp.stack([o - jj + 40, o - PC - jj + 20])]
  transfers between devices with their start and end apart: 2 -> 2, of which waited for: 0 -> 0; matrix products, arithmetic and copies ran while one was open for 34% -> 13% of each run, Pallas kernels for 5% -> 5%
where the time goes in v5:
time: 68.7 us; the launch traced here: 68.4 us
  Pallas kernels  50.7 us (74%)
  matrix products  4.56 us (7%)
  local copies, waits for them, and re-layouts  4.49 us (7%)
  starting transfers between devices  4.35 us (6%)
  other arithmetic  3.38 us (5%)
  between operations  0.89 us (1%)
    pallas_call x1, Pallas kernels, on_device(): pl.pallas_call(functools.partial(main_kernel, n, terms), out_shape=(jax.S...  47.3 us
    pallas_call x1, Pallas kernels, col_operator(): pl.pallas_call(functools.partial(band_kernel, terms), grid=(visits,), in_...  3.39 us
    ppermute x1, starting transfers between devices, on_device(): before = lax.ppermute(image[:early], 'tile', up)  3.05 us
    unnamed x10, local copies, waits for them, and re-layouts  2.62 us
    dot_general x1, matrix products, edge_operator(): jnp.einsum('vemj,vkejo->vekmo', taps, psf, precision=lax.Precision.HIGHEST)  1.58 us
  transfers between devices with their start and end apart: 2, of which 0 were waited for; matrix products, arithmetic and copies ran while one was open for 13% of the time, Pallas kernels for 5%

profile of v5, /device:TPU:0, one launch (start us, length us, event | category | flops | bytes accessed | tf_op | source)
XLA Modules:
  0.0 68.4 jit_solution(16104926077932649116)
XLA Ops:
  0.6 0.0 copy-start
  0.6 1.0 %slice.59 = f32[1,24,4096]{2,1,0:T(8,128)S(1)} slice(f32[4,24,4096]{2,1,0:T(8,128)} %image.1), slice={[0:1], [0:24], [0:4096]} | slice | bytes 786432 | tf_op jit(solution)/shard_map/slice | solution.py:294
  1.7 0.0 copy-start.3
  1.7 1.3 %collective-permute-start.1 = (f32[1,24,4096]{2,1,0:T(8,128)S(1)}, f32[1,24,4096]{2,1,0:T(8,128)S(1)}, u32[]{:S(2)}, u32[]{:S(2)}) collective-permute-start(f32[1,24,4096]{2,1,0:T(8,128)S(1)} %slice.59), channel_id=1, source_target_pairs={{1,0},{2,1},{3,2},{4,3},{5,4},{6,5},{7,6},{8,7},{9,8},{10,9},{11,1... | collective-permute-start | bytes 1179656 | tf_op jit(solution)/shard_map/ppermute | solution.py:295
  3.0 3.1 %collective-permute-start = (f32[1,24,4096]{2,1,0:T(8,128)S(1)}, f32[1,24,4096]{2,1,0:T(8,128)S(1)}, u32[]{:S(2)}, u32[]{:S(2)}) collective-permute-start(f32[1,24,4096]{2,1,0:T(8,128)S(1)} %slice.59), channel_id=1, source_target_pairs={{0,1},{1,2},{2,3},{3,4},{4,5},{5,6},{6,7},{7,8},{8,9},{9,10},{10,1... | collective-permute-start | bytes 1179656 | tf_op jit(solution)/shard_map/ppermute | solution.py:294
  6.2 0.8 %slice_bitcast_fusion.15 = (f32[4]{0:T(128)S(1)}, f32[4]{0:T(128)S(1)}) fusion(f32[4,2]{0,1:T(2,128)} %param.10), kind=kLoop, calls=%fused_computation.300 | loop fusion | bytes 64 | tf_op jit(solution)/shard_map/add | solution.py:22
  7.0 0.7 %fusion.101 = f32[128,16]{1,0:T(8,128)S(1)} fusion(s32[128]{0:T(128)} %bitcast.72), kind=kLoop, calls=%fused_computation.114 | loop fusion | flops 4096 | bytes 8704 | tf_op jit(solution)/shard_map/convert_element_type | solution.py:301
  7.8 0.1 reshape.318.hot
  7.8 0.1 fusion.226
  8.0 0.1 broadcast_divide_fusion
  8.1 1.0 %convolution_bitcast_fusion.1 = f32[4,3,24,64]{3,0,1,2:T(4,128)S(1)} fusion(s32[24,64]{1,0:T(8,128)S(1)} %subtract_add_fusion.3, f32[4,3,41]{2,0,1:T(4,128)} %param.12), kind=kOutput, calls=%fused_computation.6 | convolution fusion | flops 9131520 | bytes 81840 | tf_op jit(solution)/shard_map/vka,ima->vkim/dot_general | solution.py:49
  9.1 0.5 fusion.30
  9.7 0.4 compare_bitcast_fusion
  10.1 0.0 copy-done
  10.2 0.4 convolution_bitcast_fusion
  10.6 0.0 copy-done.3
  10.6 1.0 %convolution_bitcast_fusion.2.c_ref = f32[4,3,256]{2,1,0:T(4,128)} fusion(f32[4]{0:T(128)S(1)} %get-tuple-element.10, f32[4]{0:T(128)S(1)} %get-tuple-element.11, f32[4]{0:T(128)S(1)} %get-tuple-element.12, f32[4]{0:T(128)S(1)} %get-tuple-element.13, f32[4]{0:T(128)S(1)} %get-tuple-element.14, f32[4]{0:T(128)S(1)} %get-tuple-element.15, ...), kind=kOutput, calls=%fused_computation.7 | convolution fusion | flops 2393088 | bytes 56368 | tf_op jit(solution)/shard_map/vkb,vbl->vkl/dot_general | solution.py:105
  11.6 3.4 %shard_map.86.cols_op = bf16[4,1152,256]{2,1,0:T(8,128)(2,1)} custom-call(f32[4,3,256]{2,1,0:T(4,128)} %convolution_bitcast_fusion.2.c_ref), custom_call_target="tpu_custom_call" | custom-call | tf_op jit(solution)/shard_map/pallas_call | solution.py:106
  15.0 0.1 iota_subtract_fusion
  15.1 0.1 fusion.28.rows_op
  15.2 1.6 %fusion.8 = f32[4,2,3,128,128]{3,4,2,1,0:T(8,128)S(1)} fusion(f32[4,3,2,20,128]{4,0,1,3,2:T(4,128)S(1)} %convolution_bitcast_fusion, f32[4]{0:T(128)S(1)} %get-tuple-element.10, f32[4]{0:T(128)S(1)} %get-tuple-element.11, f32[4]{0:T(128)S(1)} %get-tuple-element.12, f32[4]{0:T(128)S(1)} %get-tuple-element.13, f32[4]{0:T(128)S(1)} %get-tuple-element.14, ...), kind=kOutput, calls=%fused_computation.24 | convolution fusion | flops 94822400 | bytes 1839232 | tf_op jit(solution)/shard_map/vemj,vkejo->vekmo/dot_general | solution.py:77
  16.8 0.3 reduce-precision_convert_fusion
  17.1 0.0 copy-start.1
  17.1 0.0 copy-start.2
  17.1 1.3 %pad_maximum_fusion.edge_op = bf16[4,2,384,256]{3,2,1,0:T(8,128)(2,1)} fusion(bf16[4,2,384,128]{3,2,1,0:T(8,128)(2,1)S(1)} %get-tuple-element.6, bf16[4,2,384,128]{3,2,1,0:T(8,128)(2,1)S(1)} %get-tuple-element.5), kind=kLoop, calls=%fused_computation.4 | loop fusion | flops 3145728 | bytes 3145728 | tf_op jit(solution)/shard_map/concatenate | solution.py:79
  18.5 0.0 collective-permute-done.1.after
  18.5 0.0 collective-permute-done.before
  18.5 0.6 copy-done.1
  19.1 0.5 copy-done.2
  19.6 47.3 %shard_map.87 = (bf16[4,24,4096]{2,1,0:T(8,128)(2,1)S(1)}, f32[1,24,128]{2,1,0:T(8,128)S(1)}) custom-call(f32[4,24,4096]{2,1,0:T(8,128)S(1)} %copy-done.1, f32[1,24,4096]{2,1,0:T(8,128)S(1)} %collective-permute-done.before, f32[1,24,4096]{2,1,0:T(8,128)S(1)} %collective-permute-done.1.after, f32[4,24,4096]{2,1,0:T(8,128)S(1)} %copy-done.2, ...), custom_call_target="tpu_custom_call" | custom-call | tf_op jit(solution)/shard_map/pallas_call | solution.py:303
  66.9 0.9 %copy.32 = bf16[4,24,4096]{2,1,0:T(8,128)(2,1)} copy(bf16[4,24,4096]{2,1,0:T(8,128)(2,1)S(1)} %get-tuple-element.46) | data formatting | bytes 1572864
  67.8 0.6 copy.33
  (17 shorter events, 0.2 us)
Async XLA Ops:
  0.6 9.5 %copy-start = (f32[4,3,41]{2,0,1:T(4,128)S(1)}, f32[4,3,41]{2,0,1:T(4,128)}, u32[]{:S(2)}) copy-start(f32[4,3,41]{2,0,1:T(4,128)} %param.13) | copy-start | bytes 5908
  1.7 8.9 %copy-start.3 = (s32[4]{0:T(128)S(1)}, s32[4]{0:T(128)}, u32[]{:S(2)}) copy-start(s32[4]{0:T(128)} %param.11) | copy-start | bytes 52
  1.7 16.8 %collective-permute-start.1 = (f32[1,24,4096]{2,1,0:T(8,128)S(1)}, f32[1,24,4096]{2,1,0:T(8,128)S(1)}, u32[]{:S(2)}, u32[]{:S(2)}) collective-permute-start(f32[1,24,4096]{2,1,0:T(8,128)S(1)} %slice.59), channel_id=1, source_target_pairs={{1,0},{2,1},{3,2},{4,3},{5,4},{6,5},{7,6},{8,7},{9,8},{10,9},{11,1... | collective-permute-start | bytes 1179656 | tf_op jit(solution)/shard_map/ppermute | solution.py:295
  3.0 15.5 %collective-permute-start = (f32[1,24,4096]{2,1,0:T(8,128)S(1)}, f32[1,24,4096]{2,1,0:T(8,128)S(1)}, u32[]{:S(2)}, u32[]{:S(2)}) collective-permute-start(f32[1,24,4096]{2,1,0:T(8,128)S(1)} %slice.59), channel_id=1, source_target_pairs={{0,1},{1,2},{2,3},{3,4},{4,5},{5,6},{6,7},{7,8},{8,9},{9,10},{10,1... | collective-permute-start | bytes 1179656 | tf_op jit(solution)/shard_map/ppermute | solution.py:294
  17.1 2.0 %copy-start.1 = (f32[4,24,4096]{2,1,0:T(8,128)S(1)}, f32[4,24,4096]{2,1,0:T(8,128)}, u32[]{:S(2)}) copy-start(f32[4,24,4096]{2,1,0:T(8,128)} %image.1) | copy-start | bytes 4718596
  17.1 2.4 %copy-start.2 = (f32[4,24,4096]{2,1,0:T(8,128)S(1)}, f32[4,24,4096]{2,1,0:T(8,128)}, u32[]{:S(2)}) copy-start(f32[4,24,4096]{2,1,0:T(8,128)} %inv_var.1) | copy-start | bytes 4718596
